TPU v7x, 32 devices: a whole 2x2x4 slice. The times are simulated.
32 devices in a mesh: row: 4 (over y, x), col: 8 (over z, core).
Axes of the slice: x: 2, y: 2, z: 4, core: 2. Of those that a mesh axis runs over, the one named last changes fastest.
Arguments:
- ainv_top: float32 [4096, 4096], P('row', 'col'), may hold values from -6 to 6
- block_owner: int32 [32], replicated, may hold values from 0 to 31, as said below
- upper_list: int32 [16, 16], P('col'), may hold values from 0 to 31, as said below
- upper_len: int32 [16], P('col'), may hold values from 12 to 16
- upper_panel: float32 [16, 2048, 128], P('col', 'row'), may hold values from -0.125 to 0.125
- upper_dinv: float32 [16, 128, 128], P('col'), may hold values from -6 to 6
- lower_len: int32 [16], P('col'), may hold values from 8 to 16, as said below
- lower_panel: float32 [16, 2048, 128], P('col', 'row'), may hold values from -0.125 to 0.125
- lower_parent: float32 [16, 128, 128], P('col'), may hold values from -0.5 to 0.5
- lower_dinv: float32 [16, 128, 128], P('col'), may hold values from -6 to 6
Outputs:
- upper_offdiag: float32 [16, 128, 4096], P('col', None, 'row')
- upper_diag: float32 [16, 128, 128], P('col')
- lower_offdiag: float32 [16, 128, 4096], P('col', None, 'row')
- lower_parent_block: float32 [16, 128, 128], P('col')
- lower_diag: float32 [16, 128, 128], P('col')
Inputs may be any that keep to these rules, and one draw needn't show every extreme that they name: `block_owner`: a permutation of the storage blocks. `upper_list`: each row holds 16 different logical top block indices; their storage blocks are exactly 2 of each run of 4 storage blocks that starts at a multiple of 4. `lower_len`: never more than upper_len of the same supernode.
All inputs are finite; a program needn't handle non-finite values.
Results may differ from a plain program's by a relative error of at most 0.0003.
Values sent between devices are 32-bit elements; how exact they have to be, the bound alone decides.
A program may use at most 192 MiB of HBM per device.

v0:
```python
import jax
import jax.numpy as jnp
from jax import lax
from jax.sharding import PartitionSpec as P

highest = lax.Precision.HIGHEST


def contract(left, right, left_dim, right_dim):
    return lax.dot_general(
        left,
        right,
        (((left_dim,), (right_dim,)), ((), ())),
        precision=highest,
        preferred_element_type=jnp.float32,
    )


def spread_panel(picked, panel, block_w):
    pieces = panel.reshape(picked.shape[1], block_w, block_w)
    dense = jnp.einsum("sp,pij->jsi", picked, pieces, precision=highest)
    return dense.reshape(block_w, picked.shape[0] * block_w)


def body(
    ainv_top,
    block_owner,
    upper_list,
    upper_len,
    upper_panel,
    upper_dinv,
    lower_len,
    lower_panel,
    lower_parent,
    lower_dinv,
):
    block_w = upper_dinv.shape[-1]
    per_col = upper_dinv.shape[0]
    local_rows = ainv_top.shape[0]
    row_blocks = local_rows // block_w
    total = block_owner.shape[0]
    panels = (
        lax.all_gather(upper_panel, "row", axis=1, tiled=True),
        lax.all_gather(lower_panel, "row", axis=1, tiled=True),
    )
    row_slots = lax.axis_index("row") * row_blocks + jnp.arange(row_blocks, dtype=jnp.int32)
    every = jnp.arange(total, dtype=jnp.int32)

    def slots_of(names):
        return jnp.sum(jnp.where(names[:, None] == every[None, :], block_owner[None, :], 0), axis=1)

    def prepare(names, upper_count, lower_count, upper_full, lower_full):
        slots = slots_of(names)
        places = jnp.arange(names.shape[0], dtype=jnp.int32)
        live_up = places < upper_count
        live_low = places < lower_count
        same = slots[None, :] == every[:, None]
        pick_up = (same & live_up[None, :]).astype(jnp.float32)
        pick_low = (same & live_low[None, :]).astype(jnp.float32)
        local_same = slots[None, :] == row_slots[:, None]
        hit_up = jnp.sum((local_same & live_up[None, :]).astype(jnp.float32), axis=1)
        hit_low = jnp.sum((local_same & live_low[None, :]).astype(jnp.float32), axis=1)
        return (
            spread_panel(pick_up, upper_full, block_w),
            spread_panel(pick_low, lower_full, block_w),
            jnp.repeat(hit_up, block_w),
            jnp.repeat(hit_low, block_w),
        )

    spread_up, spread_low, mask_up, mask_low = jax.vmap(prepare)(
        upper_list, upper_len, lower_len, panels[0], panels[1]
    )
    spread_all = jnp.concatenate(
        [
            spread_up.reshape(per_col * block_w, total * block_w),
            spread_low.reshape(per_col * block_w, total * block_w),
        ],
        axis=0,
    )
    received = lax.all_to_all(spread_all, "col", split_axis=1, concat_axis=0, tiled=True)
    products = lax.psum_scatter(
        -contract(received, ainv_top, 1, 1), "col", scatter_dimension=0, tiled=True
    )
    products = products.reshape(2, per_col, block_w, local_rows)
    first_col = lax.axis_index("row") * local_rows
    local_up = lax.dynamic_slice_in_dim(spread_up, first_col, local_rows, 2)
    local_low = lax.dynamic_slice_in_dim(spread_low, first_col, local_rows, 2)
    upper_rows = products[0] * mask_up[:, None, :]
    lower_rows = (
        products[1] - jnp.einsum("bij,bik->bjk", lower_parent, upper_rows, precision=highest)
    ) * mask_low[:, None, :]
    upper_term = jnp.einsum("bis,bjs->bij", local_up, upper_rows, precision=highest)
    cross_term = jnp.einsum("bis,bjs->bij", upper_rows, local_low, precision=highest)
    lower_term = jnp.einsum("bis,bjs->bij", local_low, lower_rows, precision=highest)
    totals = lax.psum((upper_term, cross_term, lower_term), "row")
    diag_up = upper_dinv - totals[0]
    parent_row = -(jnp.einsum("bij,bjk->bik", diag_up, lower_parent, precision=highest) + totals[1])
    diag_low = (
        lower_dinv
        - jnp.einsum("bji,bjk->bik", lower_parent, parent_row, precision=highest)
        - totals[2]
    )
    return (upper_rows, diag_up, lower_rows, parent_row, diag_low)


def solution(mesh):
    in_specs = (
        P("row", "col"),
        P(),
        P("col", None),
        P("col"),
        P("col", "row", None),
        P("col", None, None),
        P("col"),
        P("col", "row", None),
        P("col", None, None),
        P("col", None, None),
    )
    out_specs = (
        P("col", None, "row"),
        P("col", None, None),
        P("col", None, "row"),
        P("col", None, None),
        P("col", None, None),
    )
    return jax.shard_map(body, mesh=mesh, in_specs=in_specs, out_specs=out_specs, check_vma=False)
```

profile of v0, /device:TPU:16, one launch (start us, length us, event | category | flops | bytes accessed | tf_op | source)
XLA Modules:
  0.0 569.8 jit_solution(16448191348147499454)
XLA Ops:
  8.0 0.7 all-gather.5.cloned.1.call-update
  8.7 0.9 select_reduce_fusion
  9.6 0.7 iota_compare_fusion.3
  10.3 0.7 iota_compare_fusion.2
  11.1 35.2 %all-gather.3.cloned.1.call-done = f32[2,2048,128]{2,1,0:T(8,128)} async-done(((f32[2,512,128]{2,1,0:T(8,128)}), f32[2,2048,128]{2,1,0:T(8,128)}) %all-gather.3.cloned.1.call-update) | async-done | bytes 2097168 | tf_op jit(solution)/shard_map/all_gather | solution.py:43
  46.3 6.3 %convolution_bitcast_fusion.1 = f32[2,128,32,128]{1,2,3,0:T(8,128)} fusion(f32[2,16,128,128]{3,2,1,0:T(8,128)} %bitcast.66, s32[2,16]{1,0:T(2,128)S(1)} %select_reduce_fusion, pred[2,16]{1,0:T(4,128)(4,1)S(1)} %iota_compare_fusion.3), kind=kOutput, calls=%fused_computation.3 | convolution fusion | flops 201328640 | bytes 6291616 | tf_op jit(solution)/shard_map/vmap(sp,pij->jsi)/dot_general | solution.py:21
  52.6 6.2 %copy.58 = f32[2,128,32,128]{3,2,1,0:T(8,128)} copy(f32[2,128,32,128]{1,2,3,0:T(8,128)} %convolution_bitcast_fusion.1) | data formatting | bytes 8388608 | tf_op jit(solution)/shard_map/vmap(sp,pij->jsi)/transpose | solution.py:21
  58.8 4.9 concatenate.8
  63.8 19.7 %all-gather.5.cloned.1.call-done = f32[2,2048,128]{2,1,0:T(8,128)} async-done(((f32[2,512,128]{2,1,0:T(8,128)}), f32[2,2048,128]{2,1,0:T(8,128)}) %all-gather.5.cloned.1.call-update) | async-done | bytes 2097168 | tf_op jit(solution)/shard_map/all_gather | solution.py:44
  83.5 6.4 %convolution_bitcast_fusion = f32[2,128,32,128]{1,2,3,0:T(8,128)} fusion(f32[2,16,128,128]{3,2,1,0:T(8,128)} %bitcast.67, s32[2,16]{1,0:T(2,128)S(1)} %select_reduce_fusion, pred[2,16]{1,0:T(4,128)(4,1)S(1)} %iota_compare_fusion.2), kind=kOutput, calls=%fused_computation.2 | convolution fusion | flops 201328640 | bytes 6291616 | tf_op jit(solution)/shard_map/vmap(sp,pij->jsi)/dot_general | solution.py:21
  89.8 5.9 %copy.60 = f32[2,128,32,128]{3,2,1,0:T(8,128)} copy(f32[2,128,32,128]{1,2,3,0:T(8,128)} %convolution_bitcast_fusion) | data formatting | bytes 8388608 | tf_op jit(solution)/shard_map/vmap(sp,pij->jsi)/transpose | solution.py:21
  95.7 4.9 concatenate.9
  100.6 4.4 pad_maximum_fusion
  105.1 8.1 %copy.61 = f32[512,8,512]{2,0,1:T(8,128)} copy(f32[512,8,512]{2,1,0:T(8,128)S(1)} %pad_maximum_fusion) | data formatting | bytes 16777216 | tf_op jit(solution)/shard_map/concatenate | solution.py:73
  113.1 186.2 %all_to_all.16 = f32[512,8,512]{2,0,1:T(8,128)S(1)} all-to-all(f32[512,8,512]{2,0,1:T(8,128)} %copy.61), channel_id=1, replica_groups=mesh['row'=4,'col'=8] {'col'}, dimensions={1} | all-to-all | bytes 16777216 | tf_op jit(solution)/shard_map/all_to_all | solution.py:80
  299.3 29.9 %convolution_negate_fusion = f32[4096,1024]{1,0:T(8,128)} fusion(f32[4096,512]{1,0:T(8,128)S(1)} %bitcast.60, f32[1024,512]{1,0:T(8,128)S(1)} %copy-done), kind=kOutput, calls=%fused_computation | convolution fusion | flops 25773998080 | bytes 27262976 | tf_op jit(solution)/shard_map/dot_general | solution.py:10
  329.9 6.9 %copy.66 = f32[2,128,32,128]{1,3,2,0:T(8,128)} copy(f32[2,128,32,128]{1,2,3,0:T(8,128)} %convolution_bitcast_fusion) | data formatting | bytes 8388608 | tf_op jit(solution)/shard_map/vmap(sp,pij->jsi)/transpose | solution.py:21
  336.8 4.4 copy.62
  341.2 154.3 %reduce-scatter.2.cloned.1.call-done = f32[512,1024]{1,0:T(8,128)} async-done(((f32[4096,1024]{1,0:T(8,128)}), f32[512,1024]{1,0:T(8,128)}) %reduce-scatter.2.cloned.1.call-update) | async-done | bytes 2097168 | tf_op jit(solution)/shard_map/reduce_scatter | solution.py:81
  495.5 1.8 fusion.26
  497.3 1.3 copy.65
  498.8 3.5 fusion.9
  502.3 2.0 fusion.3
  504.3 1.0 copy-done.4
  505.2 3.8 fusion.11
  509.0 3.7 fusion.7
  512.9 2.5 copy.72
  515.5 43.1 %all-reduce.3.cloned.1.call-done = (f32[2,128,128]{2,1,0:T(8,128)}, f32[2,128,128]{2,1,0:T(8,128)}, f32[2,128,128]{1,2,0:T(8,128)}) async-done(((f32[2,128,128]{2,1,0:T(8,128)}, f32[2,128,128]{2,1,0:T(8,128)}, f32[2,128,128]{1,2,0:T(8,128)}), (f32[2,128,128]{2,1,0:T(8,128)}, f32[2,128,128]{2,1,0:T(8,128)}, f32[2,128,128]{1,2,0:T(8,128)})) %all-reduce.3.cloned.1.call-update) | async-done | bytes 393232 | tf_op jit(solution)/shard_map/psum | solution.py:95
  558.6 0.9 sub.12
  559.5 1.2 fusion.6
  560.8 1.3 fusion.5
  562.1 0.8 copy.73
  (36 shorter events, 1.7 us)
Async XLA Ops:
  7.2 292.2 %copy-start = (f32[1024,512]{1,0:T(8,128)S(1)}, f32[1024,512]{1,0:T(8,128)}, u32[]{:S(2)}) copy-start(f32[1024,512]{1,0:T(8,128)} %param.10) | copy-start | bytes 6291460
  7.2 39.1 %all-gather.3.cloned.1.call-start = ((), (), s32[]{:S(2)}) async-start(), calls=%async_computation.2 | async-start | bytes 2621440 | tf_op jit(solution)/shard_map/all_gather | solution.py:43
  7.9 75.6 %all-gather.5.cloned.1.call-start = ((), (), s32[]{:S(2)}) async-start(), calls=%async_computation.3 | async-start | bytes 2621440 | tf_op jit(solution)/shard_map/all_gather | solution.py:44
  8.7 486.9 %reduce-scatter.2.cloned.1.call-start = ((), (), s32[]{:S(2)}) async-start(), calls=%async_computation.4 | async-start | bytes 18874368 | tf_op jit(solution)/shard_map/reduce_scatter | solution.py:81
  329.3 229.3 %all-reduce.3.cloned.1.call-start = ((), (), s32[]{:S(2)}) async-start(), calls=%async_computation.5 | async-start | bytes 786432 | tf_op jit(solution)/shard_map/psum | solution.py:95
  329.9 6.9 %copy-start.2 = (f32[2,128,32,128]{1,2,3,0:T(8,128)S(1)}, f32[2,128,32,128]{1,2,3,0:T(8,128)}, u32[]{:S(2)}) copy-start(f32[2,128,32,128]{1,2,3,0:T(8,128)} %convolution_bitcast_fusion.1) | copy-start | bytes 12582916
  497.3 4.9 copy-start.6
  498.6 3.6 copy-start.5
  498.8 14.0 %copy-start.3 = (f32[2,128,1024]{2,1,0:T(8,128)}, f32[2,128,1024]{2,1,0:T(8,128)S(1)}, u32[]{:S(2)}) copy-start(f32[2,128,1024]{2,1,0:T(8,128)S(1)} %broadcast_multiply_fusion) | copy-start | bytes 3145732
  502.3 10.6 %copy-start.10 = (f32[2,128,128]{2,1,0:T(8,128)S(1)}, f32[2,128,128]{2,1,0:T(8,128)}, u32[]{:S(2)}) copy-start(f32[2,128,128]{2,1,0:T(8,128)} %param.19) | copy-start | bytes 393220
  502.3 60.6 %copy-start.1 = (f32[1024,512]{1,0:T(8,128)S(1)}, f32[1024,512]{1,0:T(8,128)}, u32[]{:S(2)}) copy-start(f32[1024,512]{1,0:T(8,128)} %param.10) | copy-start | bytes 6291460
  504.3 1.0 copy-start.4
  505.2 53.3 %copy-start.9 = (f32[2,128,128]{2,1,0:T(8,128)S(1)}, f32[2,128,128]{2,1,0:T(8,128)}, u32[]{:S(2)}) copy-start(f32[2,128,128]{2,1,0:T(8,128)} %param.15) | copy-start | bytes 393220
  559.5 3.4 copy-start.7
  560.7 2.1 copy-start.8
Sparse Core Ops, SparseCore 0:
  9.9 36.3 all-gather.2
  48.1 35.2 all-gather.4
  329.4 166.1 reduce-scatter.1
  512.9 45.5 all-reduce.2
where the time goes:
time: 575 us; the launch traced here: 570 us
  waiting for transfers between devices  254 us (44%)
  blocking collectives  186 us (32%)
  matrix products  58.2 us (10%)
  local copies, waits for them, and re-layouts  48.9 us (9%)
  between operations  14.4 us (3%)
  other arithmetic  7.97 us (1%)
    all_to_all x1, blocking collectives, body(): lax.all_to_all(spread_all, 'col', split_axis=1, concat_axis=0, tiled=True)  186 us
    reduce_scatter x1, waiting for transfers between devices, body(): lax.psum_scatter(-contract(received, ainv_top, 1, 1), 'col', scatter_dime...  154 us
    psum x1, waiting for transfers between devices, body(): totals = lax.psum((upper_term, cross_term, lower_term), 'row')  43.1 us
    all_gather x1, waiting for transfers between devices, body(): lax.all_gather(upper_panel, 'row', axis=1, tiled=True)  35.2 us
    dot_general x1, matrix products, contract(): lax.dot_general(left, right, (((left_dim,), (right_dim,)), ((), ())), pre...  29.9 us
    transpose x4, local copies, waits for them, and re-layouts, spread_panel(): dense = jnp.einsum('sp,pij->jsi', picked, pieces, precision=highest)  23.4 us
    all_gather x1, waiting for transfers between devices, body(): lax.all_gather(lower_panel, 'row', axis=1, tiled=True)  19.7 us
    concatenate x3, local copies, waits for them, and re-layouts, body(): jnp.concatenate([spread_up.reshape(per_col * block_w, total * block_w), s...  17.9 us
  transfers between devices with their start and end apart: 4, of which 4 were waited for; matrix products, arithmetic and copies ran while one was open for 6% of the time, Pallas kernels for 0%

commit v1 on v0

v1 whole, which is shorter than its diff:
```python
import functools

import jax
import jax.numpy as jnp
from jax import lax
from jax.experimental import pallas as pl
from jax.experimental.pallas import tpu as pltpu
from jax.sharding import PartitionSpec as P

highest = lax.Precision.HIGHEST
VMEM = pltpu.VMEM
SMEM = pltpu.SMEM


def nt(left, right):
    return lax.dot_general(
        left, right, (((1,), (1,)), ((), ())), precision=highest, preferred_element_type=jnp.float32
    )


def tn(left, right):
    return lax.dot_general(
        left, right, (((0,), (0,)), ((), ())), precision=highest, preferred_element_type=jnp.float32
    )


def split_bf16(value):
    high = value.astype(jnp.bfloat16)
    low = (value - high.astype(jnp.float32)).astype(jnp.bfloat16)
    return high, low


def pick_kernel(order_ref, live_ref, panel_ref, out_ref):
    for place in range(out_ref.shape[0]):
        block = panel_ref[order_ref[place]]
        kept = jnp.where(live_ref[place] > 0, block, 0.0)
        out_ref[place] = kept.T


def product_kernel(per_col, row_ref, col_ref, ainv_ref, panel_ref, out_ref, high_ref, low_ref):
    col_blocks, row_blocks, width, _ = high_ref.shape
    step = pl.program_id(0)

    @pl.when(step == 0)
    def _():
        for cb in range(col_blocks):
            for rb in range(row_blocks):
                block = ainv_ref[rb * width:(rb + 1) * width, cb * width:(cb + 1) * width]
                high, low = split_bf16(block)
                high_ref[cb, rb] = high
                low_ref[cb, rb] = low

    n_row, _, col_live, piece, _ = panel_ref.shape
    row_live = out_ref.shape[3] // width
    parts = n_row // (2 * per_col)
    for node in range(per_col):
        rows = []
        for panel in range(2):
            for part in range(parts):
                source = (panel * per_col + node) * parts + part
                rows.append(jnp.concatenate([panel_ref[source, 0, s] for s in range(col_live)], axis=1))
        left = jnp.concatenate(rows, axis=0)
        left_high, left_low = split_bf16(left)
        left_all = jnp.concatenate([left_high, left_high, left_low], axis=1)
        at = step * per_col + node
        for rb in range(row_live):
            row = row_ref[at, rb]
            cols = [col_ref[at, s] for s in range(col_live)]
            high = [high_ref[cb, row] for cb in cols]
            low = [low_ref[cb, row] for cb in cols]
            right = jnp.concatenate(high + low + high, axis=1)
            total = lax.dot_general(
                left_all, right, (((1,), (1,)), ((), ())), preferred_element_type=jnp.float32
            )
            for panel in range(2):
                out_ref[0, panel * per_col + node, :, rb * width:(rb + 1) * width] = (
                    -total[panel * width:(panel + 1) * width]
                )


def finish_kernel(per_col, at_ref, up_ref, low_ref, sums_ref, local_ref, parent_ref,
                  up_off_ref, low_off_ref, terms_ref):
    width = parent_ref.shape[-1]
    n_row, count, piece, _ = local_ref.shape
    parts = n_row // (2 * per_col)
    up_off_ref[...] = jnp.zeros_like(up_off_ref)
    low_off_ref[...] = jnp.zeros_like(low_off_ref)

    def whole(combo, place):
        return jnp.concatenate([local_ref[combo * parts + part, place] for part in range(parts)], axis=0)

    for node in range(per_col):
        upper_term = jnp.zeros((width, width), jnp.float32)
        cross_term = jnp.zeros((width, width), jnp.float32)
        lower_term = jnp.zeros((width, width), jnp.float32)
        for place in range(count):
            span = slice(place * width, (place + 1) * width)
            upper = jnp.where(up_ref[node, place] > 0, sums_ref[node, :, span], 0.0)
            lower = sums_ref[per_col + node, :, span] - tn(parent_ref[node], upper)
            lower = jnp.where(low_ref[node, place] > 0, lower, 0.0)
            at = pl.ds(pl.multiple_of(at_ref[node, place] * width, width), width)
            up_off_ref[node, :, at] = upper
            low_off_ref[node, :, at] = lower
            local_up = whole(node, place)
            local_low = whole(per_col + node, place)
            upper_term += nt(local_up, upper)
            cross_term += nt(upper, local_low)
            lower_term += nt(local_low, lower)
        terms_ref[0, node] = upper_term
        terms_ref[1, node] = cross_term
        terms_ref[2, node] = lower_term


def body(
    n_row,
    n_col,
    ainv_top,
    block_owner,
    upper_list,
    upper_len,
    upper_panel,
    upper_dinv,
    lower_len,
    lower_panel,
    lower_parent,
    lower_dinv,
):
    width = upper_dinv.shape[-1]
    per_col = upper_dinv.shape[0]
    local_rows, local_cols = ainv_top.shape
    row_blocks = local_rows // width
    col_blocks = local_cols // width
    row_live = row_blocks // 2
    col_live = col_blocks // 2
    total = block_owner.shape[0]
    listed = upper_list.shape[1]
    mine = listed // n_row
    combos = 2 * per_col
    parts = n_row // combos
    piece = width // parts
    params = pltpu.CompilerParams(vmem_limit_bytes=40 * 1024 * 1024)
    here = lax.axis_index("row")

    every = jnp.arange(total, dtype=jnp.int32)
    places = jnp.arange(listed, dtype=jnp.int32)
    slots = jnp.sum(
        jnp.where(upper_list[:, :, None] == every, block_owner[None, None, :], 0), axis=2
    )
    rank = jnp.sum((slots[:, None, :] < slots[:, :, None]).astype(jnp.int32), axis=2)
    hit = rank[:, :, None] == places[None, None, :]
    order = jnp.sum(jnp.where(hit, places[None, :, None], 0), axis=1)
    sorted_slots = jnp.sum(jnp.where(hit, slots[:, :, None], 0), axis=1)
    live_up = (order < upper_len[:, None]).astype(jnp.int32)
    live_low = (order < lower_len[:, None]).astype(jnp.int32)
    all_slots = lax.all_gather(sorted_slots, "col", axis=0, tiled=True)

    panels = jnp.concatenate([upper_panel, lower_panel], axis=0)
    panels = panels.reshape(combos, mine, width, parts, piece)
    panels = panels.transpose(0, 3, 1, 2, 4).reshape(n_row, mine, width, piece)
    whole = lax.all_to_all(panels, "row", split_axis=0, concat_axis=0, tiled=True)
    whole = whole.reshape(listed, width, piece)
    combo = here // parts
    node = combo % per_col
    live_all = jnp.concatenate([live_up, live_low], axis=0)
    spread = pl.pallas_call(
        pick_kernel,
        out_shape=jax.ShapeDtypeStruct((listed, piece, width), jnp.float32),
        in_specs=[pl.BlockSpec(memory_space=SMEM)] * 2 + [pl.BlockSpec(memory_space=VMEM)],
        out_specs=pl.BlockSpec(memory_space=VMEM),
        compiler_params=params,
        name="pick",
    )(order[node], live_all[combo], whole)

    landed = lax.all_to_all(
        spread.reshape(n_col, col_live, piece, width), "col", split_axis=0, concat_axis=0, tiled=True
    )
    gathered = lax.all_gather(landed, "row", axis=0, tiled=False)
    row_at = lax.dynamic_slice_in_dim(all_slots, here * row_live, row_live, 1) - here * row_blocks
    col_here = lax.axis_index("col")
    col_at = lax.dynamic_slice_in_dim(all_slots, col_here * col_live, col_live, 1) - col_here * col_blocks
    live_width = row_live * width
    partial = pl.pallas_call(
        functools.partial(product_kernel, per_col),
        grid=(n_col,),
        out_shape=jax.ShapeDtypeStruct((n_col, combos, width, live_width), jnp.float32),
        in_specs=[
            pl.BlockSpec(memory_space=SMEM),
            pl.BlockSpec(memory_space=SMEM),
            pl.BlockSpec((local_rows, local_cols), lambda c: (0, 0)),
            pl.BlockSpec((n_row, 1, col_live, piece, width), lambda c: (0, c, 0, 0, 0)),
        ],
        out_specs=pl.BlockSpec((1, combos, width, live_width), lambda c: (c, 0, 0, 0)),
        scratch_shapes=[
            VMEM((col_blocks, row_blocks, width, width), jnp.bfloat16),
            VMEM((col_blocks, row_blocks, width, width), jnp.bfloat16),
        ],
        compiler_params=params,
        name="products",
    )(row_at, col_at, ainv_top, gathered)
    local = lax.all_to_all(
        spread.reshape(n_row, row_live, piece, width), "row", split_axis=0, concat_axis=0, tiled=True
    )
    sums = lax.psum_scatter(partial, "col", scatter_dimension=0, tiled=True)[0]

    mine_at = lax.dynamic_slice_in_dim(sorted_slots, here * row_live, row_live, 1) - here * row_blocks
    mine_up = lax.dynamic_slice_in_dim(live_up, here * row_live, row_live, 1)
    mine_low = lax.dynamic_slice_in_dim(live_low, here * row_live, row_live, 1)
    upper_rows, lower_rows, terms = pl.pallas_call(
        functools.partial(finish_kernel, per_col),
        out_shape=(
            jax.ShapeDtypeStruct((per_col, width, local_rows), jnp.float32),
            jax.ShapeDtypeStruct((per_col, width, local_rows), jnp.float32),
            jax.ShapeDtypeStruct((3, per_col, width, width), jnp.float32),
        ),
        in_specs=[pl.BlockSpec(memory_space=SMEM)] * 3 + [pl.BlockSpec(memory_space=VMEM)] * 3,
        out_specs=(pl.BlockSpec(memory_space=VMEM),) * 3,
        compiler_params=params,
        name="finish",
    )(mine_at, mine_up, mine_low, sums, local, lower_parent)
    totals = lax.psum(terms, "row")
    diag_up = upper_dinv - totals[0]
    parent_row = -(jnp.einsum("bij,bjk->bik", diag_up, lower_parent, precision=highest) + totals[1])
    diag_low = (
        lower_dinv
        - jnp.einsum("bji,bjk->bik", lower_parent, parent_row, precision=highest)
        - totals[2]
    )
    return (upper_rows, diag_up, lower_rows, parent_row, diag_low)


def solution(mesh):
    in_specs = (
        P("row", "col"),
        P(),
        P("col", None),
        P("col"),
        P("col", "row", None),
        P("col", None, None),
        P("col"),
        P("col", "row", None),
        P("col", None, None),
        P("col", None, None),
    )
    out_specs = (
        P("col", None, "row"),
        P("col", None, None),
        P("col", None, "row"),
        P("col", None, None),
        P("col", None, None),
    )
    inner = functools.partial(body, mesh.shape["row"], mesh.shape["col"])
    return jax.shard_map(inner, mesh=mesh, in_specs=in_specs, out_specs=out_specs, check_vma=False)
```

time: 575 us -> 276 us (0.48)
  blocking collectives: 186 us -> 38.3 us
  waiting for transfers between devices: 254 us -> 185 us
  matrix products: 58.2 us -> 3.22 us
  local copies, waits for them, and re-layouts: 48.9 us -> 3.56 us
  Pallas kernels: 0 us -> 17.8 us
  starting transfers between devices: 0.41 us -> 7.59 us
    all_to_all x1, blocking collectives: 186 us -> 28.6 us  [body(): lax.all_to_all(spread.reshape(n_col, col_live, piece, width), 'col', spli...]
    reduce_scatter x1, waiting for transfers between devices: 154 us -> 69.6 us  [body(): sums = lax.psum_scatter(partial, 'col', scatter_dimension=0, tiled=True)[0]]
    dot_general x7 -> x0, matrix products: 55.6 us -> none  [the longest x1 29.9 us: contract(): lax.dot_general(left, right, (((left_dim,), (right_dim,)), ((), ())), pre...]
    all_to_all x0 -> x2, waiting for transfers between devices: none -> 26.7 us  [the longest x1 13.7 us: body(): lax.all_to_all(spread.reshape(n_row, row_live, piece, width), 'row', spli...]
    transpose x4 -> x0, local copies, waits for them, and re-layouts: 23.4 us -> none  [spread_panel(): dense = jnp.einsum('sp,pij->jsi', picked, pieces, precision=highest)]
    concatenate x3 -> x0, local copies, waits for them, and re-layouts: 17.9 us -> none  [body(): jnp.concatenate([spread_up.reshape(per_col * block_w, total * block_w), s...]
    pallas_call x0 -> x3, Pallas kernels: none -> 17.8 us  [the longest x1 10.4 us: body(): pl.pallas_call(functools.partial(product_kernel, per_col), grid=(n_col,),...]
    all_gather x2 -> x1, waiting for transfers between devices: 54.9 us -> 43.7 us  [body(): gathered = lax.all_gather(landed, 'row', axis=0, tiled=False)]
  transfers between devices with their start and end apart: 4 -> 5, of which waited for: 4 -> 5; matrix products, arithmetic and copies ran while one was open for 6% -> 0% of each run, Pallas kernels for 0% -> 0%
where the time goes in v1:
time: 276 us; the launch traced here: 273 us
  waiting for transfers between devices  185 us (67%)
  blocking collectives  38.3 us (14%)
  Pallas kernels  17.8 us (6%)
  between operations  13.9 us (5%)
  starting transfers between devices  7.59 us (3%)
  other arithmetic  3.96 us (1%)
  local copies, waits for them, and re-layouts  3.56 us (1%)
  matrix products  3.22 us (1%)
    reduce_scatter x1, waiting for transfers between devices, body(): sums = lax.psum_scatter(partial, 'col', scatter_dimension=0, tiled=True)[0]  69.6 us
    psum x1, waiting for transfers between devices, body(): totals = lax.psum(terms, 'row')  45.1 us
    all_gather x1, waiting for transfers between devices, body(): gathered = lax.all_gather(landed, 'row', axis=0, tiled=False)  43.7 us
    all_to_all x1, blocking collectives, body(): lax.all_to_all(spread.reshape(n_col, col_live, piece, width), 'col', spli...  28.6 us
    all_to_all x1, waiting for transfers between devices, body(): lax.all_to_all(spread.reshape(n_row, row_live, piece, width), 'row', spli...  13.7 us
    all_to_all x1, waiting for transfers between devices, body(): lax.all_to_all(panels, 'row', split_axis=0, concat_axis=0, tiled=True)  13.1 us
    pallas_call x1, Pallas kernels, body(): pl.pallas_call(functools.partial(product_kernel, per_col), grid=(n_col,),...  10.4 us
    all_gather x1, blocking collectives, body(): all_slots = lax.all_gather(sorted_slots, 'col', axis=0, tiled=True)  9.7 us
  transfers between devices with their start and end apart: 5, of which 5 were waited for; matrix products, arithmetic and copies ran while one was open for 0% of the time, Pallas kernels for 0%

profile of v1, /device:TPU:16, one launch (start us, length us, event | category | flops | bytes accessed | tf_op | source)
XLA Modules:
  0.0 273.5 jit_solution(1585306314961221899)
XLA Ops:
  7.2 2.3 pad_maximum_fusion
  9.5 3.8 %all-to-all-start = ((f32[4,4,128,128]{3,2,1,0:T(8,128)}), f32[4,4,128,128]{3,2,1,0:T(8,128)S(1)}, u32[]{:S(2)}, u32[]{:S(2)}) async-start(f32[4,4,128,128]{3,2,1,0:T(8,128)} %bitcast.37), calls=%async_computation | async-start | bytes 2097152 | tf_op jit(solution)/shard_map/all_to_all | solution.py:160
  13.3 0.2 select_reduce_fusion.2
  13.5 0.2 convert_reduce_fusion
  13.7 0.1 select_reduce_fusion
  13.8 0.1 compare_convert_fusion
  13.9 13.1 %all-to-all-done = f32[4,4,128,128]{3,2,1,0:T(8,128)S(1)} async-done(((f32[4,4,128,128]{3,2,1,0:T(8,128)}), f32[4,4,128,128]{3,2,1,0:T(8,128)S(1)}, u32[]{:S(2)}, u32[]{:S(2)}) %all-to-all-start) | async-done | bytes 1048608 | tf_op jit(solution)/shard_map/all_to_all | solution.py:160
  27.0 1.9 pick.1
  28.9 28.6 %all_to_all.15 = f32[8,2,128,128]{3,2,1,0:T(8,128)} all-to-all(f32[8,2,128,128]{3,2,1,0:T(8,128)} %bitcast.6), channel_id=1, replica_groups=mesh['row'=4,'col'=8] {'col'}, dimensions={0} | all-to-all | bytes 2097152 | tf_op jit(solution)/shard_map/all_to_all | solution.py:174
  57.5 0.0 all-gather.4.cloned.1.call-update
  57.5 0.0 reduce-scatter.2.cloned.1.call-start
  57.5 9.7 %all-gather.1 = s32[8,2,16]{2,1,0:T(2,128)S(1)} all-gather(s32[1,2,16]{2,1,0:T(2,128)S(1)} %bitcast.40), channel_id=1, replica_groups=mesh['row'=4,'col'=8] {'col'}, dimensions={0}, use_global_device_ids=true | all-gather | bytes 1152 | tf_op jit(solution)/shard_map/all_gather | solution.py:155
  67.2 0.1 dynamic-slice_subtract_fusion.col_ref
  67.3 0.1 dynamic-slice_subtract_fusion.1.row_ref
  67.4 43.7 %all-gather.4.cloned.1.call-done = f32[32,2,128,128]{3,2,1,0:T(8,128)} async-done(((f32[8,2,128,128]{3,2,1,0:T(8,128)}), f32[32,2,128,128]{3,2,1,0:T(8,128)}) %all-gather.4.cloned.1.call-update) | async-done | bytes 4194320 | tf_op jit(solution)/shard_map/all_gather | solution.py:177
  111.1 2.2 copy-done
  113.3 10.4 %products.1 = f32[8,4,128,512]{3,2,1,0:T(8,128)} custom-call(s32[16,4]{1,0:T(8,128)S(1)} %dynamic-slice_subtract_fusion.1.row_ref, s32[16,2]{1,0:T(8,128)S(1)} %dynamic-slice_subtract_fusion.col_ref, f32[1024,512]{1,0:T(8,128)S(1)} %copy-done.1, f32[4,8,2,128,128]{4,3,2,1,0:T(8,128)S(1)} %bitcast.35), custom_call_target="tpu_custom_call" | custom-call | tf_op jit(solution)/shard_map/products/pallas_call | solution.py:182
  123.7 0.0 reduce-scatter.2.cloned.1.call-update
  123.8 3.7 %all-to-all-start.2 = ((f32[4,4,128,128]{3,2,1,0:T(8,128)}), f32[4,4,128,128]{3,2,1,0:T(8,128)S(1)}, u32[]{:S(2)}, u32[]{:S(2)}) async-start(f32[4,4,128,128]{3,2,1,0:T(8,128)} %bitcast.9), calls=%async_computation.3 | async-start | bytes 2097152 | tf_op jit(solution)/shard_map/all_to_all | solution.py:200
  127.4 0.0 all-reduce.2.cloned.1.call-start
  127.5 0.1 fusion.4.at_ref
  127.5 0.1 constant_dynamic-slice_fusion.1
  127.6 13.7 %all-to-all-done.2.local_ref = f32[4,4,128,128]{3,2,1,0:T(8,128)S(1)} async-done(((f32[4,4,128,128]{3,2,1,0:T(8,128)}), f32[4,4,128,128]{3,2,1,0:T(8,128)S(1)}, u32[]{:S(2)}, u32[]{:S(2)}) %all-to-all-start.2) | async-done | bytes 1048608 | tf_op jit(solution)/shard_map/all_to_all | solution.py:200
  141.3 69.6 %reduce-scatter.2.cloned.1.call-done = f32[1,4,128,512]{3,2,1,0:T(8,128)} async-done(((f32[8,4,128,512]{3,2,1,0:T(8,128)}), f32[1,4,128,512]{3,2,1,0:T(8,128)}) %reduce-scatter.2.cloned.1.call-update) | async-done | bytes 1048592 | tf_op jit(solution)/shard_map/reduce_scatter | solution.py:203
  210.9 1.2 copy-done.3
  212.2 5.5 %finish.1 = (f32[2,128,1024]{2,1,0:T(8,128)}, f32[2,128,1024]{2,1,0:T(8,128)}, f32[3,2,128,128]{3,2,1,0:T(8,128)}) custom-call(s32[2,4]{1,0:T(2,128)S(1)} %fusion.4.at_ref, s32[2,4]{1,0:T(2,128)S(1)} %get-tuple-element.16.up_ref, s32[2,4]{1,0:T(2,128)S(1)} %get-tuple-element.15.low_ref, f32[4,128,512]{2,1,0:T(8,128)S(1)} %bitcast.36, ...), custom_call_target="tpu_custom_call" | custom-call | tf_op jit(solution)/shard_map/finish/pallas_call | solution.py:208
  217.6 0.0 all-reduce.2.cloned.1.call-update
  217.7 45.1 %all-reduce.2.cloned.1.call-done = f32[3,2,128,128]{3,2,1,0:T(8,128)} async-done(((f32[3,2,128,128]{3,2,1,0:T(8,128)}), f32[3,2,128,128]{3,2,1,0:T(8,128)}) %all-reduce.2.cloned.1.call-update) | async-done | bytes 393232 | tf_op jit(solution)/shard_map/psum | solution.py:220
  262.8 0.9 fusion.3
  263.7 0.0 copy-start.4
  263.7 1.2 fusion.2
  264.9 2.0 fusion.1
  (25 shorter events, 0.1 us)
Async XLA Ops:
  7.2 6.2 %copy-start.8 = (s32[2,16]{1,0:T(2,128)S(1)}, s32[2,16]{1,0:T(2,128)}, u32[]{:S(2)}) copy-start(s32[2,16]{1,0:T(2,128)} %param.12) | copy-start | bytes 388
  7.2 6.1 %copy-start.9 = (s32[32]{0:T(128)S(1)}, s32[32]{0:T(128)}, u32[]{:S(2)}) copy-start(s32[32]{0:T(128)} %param.11) | copy-start | bytes 388
  7.2 6.6 %copy-start.10 = (s32[2]{0:T(128)S(1)}, s32[2]{0:T(128)}, u32[]{:S(2)}) copy-start(s32[2]{0:T(128)} %param.16) | copy-start | bytes 28
  7.2 6.6 %copy-start.11 = (s32[2]{0:T(128)S(1)}, s32[2]{0:T(128)}, u32[]{:S(2)}) copy-start(s32[2]{0:T(128)} %param.13) | copy-start | bytes 28
  9.5 101.6 %copy-start.1 = (f32[1024,512]{1,0:T(8,128)S(1)}, f32[1024,512]{1,0:T(8,128)}, u32[]{:S(2)}) copy-start(f32[1024,512]{1,0:T(8,128)} %ainv_ref.1) | copy-start | bytes 6291460
  9.5 17.5 %all-to-all-start = ((f32[4,4,128,128]{3,2,1,0:T(8,128)}), f32[4,4,128,128]{3,2,1,0:T(8,128)S(1)}, u32[]{:S(2)}, u32[]{:S(2)}) async-start(f32[4,4,128,128]{3,2,1,0:T(8,128)} %bitcast.37), calls=%async_computation | async-start | bytes 2097152 | tf_op jit(solution)/shard_map/all_to_all | solution.py:160
  13.3 97.8 %all-gather.4.cloned.1.call-start = ((), (), s32[]{:S(2)}) async-start(), calls=%async_computation.6 | async-start | bytes 5242880 | tf_op jit(solution)/shard_map/all_gather | solution.py:177
  57.5 153.5 %reduce-scatter.2.cloned.1.call-start = ((), (), s32[]{:S(2)}) async-start(), calls=%async_computation.4 | async-start | bytes 9437184 | tf_op jit(solution)/shard_map/reduce_scatter | solution.py:203
  111.1 2.2 copy-start
  123.7 87.2 %copy-start.2 = (f32[2,128,128]{2,1,0:T(8,128)S(1)}, f32[2,128,128]{2,1,0:T(8,128)}, u32[]{:S(2)}) copy-start(f32[2,128,128]{2,1,0:T(8,128)} %parent_ref.1) | copy-start | bytes 393220
  123.7 139.0 %copy-start.6 = (f32[2,128,128]{2,1,0:T(8,128)S(1)}, f32[2,128,128]{2,1,0:T(8,128)}, u32[]{:S(2)}) copy-start(f32[2,128,128]{2,1,0:T(8,128)} %param.15) | copy-start | bytes 393220
  123.7 141.2 %copy-start.7 = (f32[2,128,128]{2,1,0:T(8,128)S(1)}, f32[2,128,128]{2,1,0:T(8,128)}, u32[]{:S(2)}) copy-start(f32[2,128,128]{2,1,0:T(8,128)} %param.19) | copy-start | bytes 393220
  123.8 17.5 %all-to-all-start.2 = ((f32[4,4,128,128]{3,2,1,0:T(8,128)}), f32[4,4,128,128]{3,2,1,0:T(8,128)S(1)}, u32[]{:S(2)}, u32[]{:S(2)}) async-start(f32[4,4,128,128]{3,2,1,0:T(8,128)} %bitcast.9), calls=%async_computation.3 | async-start | bytes 2097152 | tf_op jit(solution)/shard_map/all_to_all | solution.py:200
  127.4 135.3 %all-reduce.2.cloned.1.call-start = ((), (), s32[]{:S(2)}) async-start(), calls=%async_computation.5 | async-start | bytes 786432 | tf_op jit(solution)/shard_map/psum | solution.py:220
  210.9 1.2 copy-start.3
  263.7 3.3 %copy-start.4 = (f32[2,128,128]{2,1,0:T(8,128)}, f32[2,128,128]{2,1,0:T(8,128)S(1)}, u32[]{:S(2)}) copy-start(f32[2,128,128]{2,1,0:T(8,128)S(1)} %fusion.3) | copy-start | bytes 393220
  264.9 2.0 copy-start.5
Sparse Core Ops, SparseCore 0:
  57.6 53.4 all-gather.3
  123.8 87.0 reduce-scatter.1
  217.8 44.9 all-reduce.1

commit v2 on v1

v2 whole, which is shorter than its diff:
```python
import functools

import jax
import jax.numpy as jnp
from jax import lax
from jax.experimental import pallas as pl
from jax.experimental.pallas import tpu as pltpu
from jax.sharding import PartitionSpec as P

highest = lax.Precision.HIGHEST
VMEM = pltpu.VMEM
SMEM = pltpu.SMEM


def nt(left, right):
    return lax.dot_general(
        left, right, (((1,), (1,)), ((), ())), precision=highest, preferred_element_type=jnp.float32
    )


def nn(left, right):
    return lax.dot_general(
        left, right, (((1,), (0,)), ((), ())), precision=highest, preferred_element_type=jnp.float32
    )


def tn(left, right):
    return lax.dot_general(
        left, right, (((0,), (0,)), ((), ())), precision=highest, preferred_element_type=jnp.float32
    )


def split_bf16(value):
    high = value.astype(jnp.bfloat16)
    low = (value - high.astype(jnp.float32)).astype(jnp.bfloat16)
    return high, low


def mega_kernel(
    per_col, n_row, n_col,
    order_ref, live_ref, row_ref, col_ref, at_ref, up_ref, low_ref,
    panels_ref, ainv_ref, parent_ref, updinv_ref, lowdinv_ref,
    up_off_ref, up_diag_ref, low_off_ref, prow_ref, low_diag_ref,
    whole, spread, gathered, high_ref, low_part_ref, own, away, mate, line, local, terms, landed, totals,
    a_send, a_recv, c_send, c_recv, g_send, g_recv, l_send, l_recv,
    s_send, s_recv, z_send, z_recv, t_send, t_recv,
):
    me_r = lax.axis_index("row")
    me_c = lax.axis_index("col")
    chips = n_col // 2
    z = me_c // 2
    core = me_c % 2
    sibling = me_c + 1 - 2 * core
    combos = 2 * per_col
    parts = n_row // combos
    mine = panels_ref.shape[1]
    col_blocks, row_blocks, width, _ = high_ref.shape
    col_live = gathered.shape[2]
    row_live = local.shape[1]

    def remote(src, dst, send, recv, target):
        return pltpu.make_async_remote_copy(
            src_ref=src, dst_ref=dst, send_sem=send, recv_sem=recv,
            device_id=target, device_id_type=pl.DeviceIdType.MESH,
        )

    barrier = pltpu.get_barrier_semaphore()
    for d in range(1, n_row):
        pl.semaphore_signal(barrier, inc=1, device_id={"row": (me_r + d) % n_row},
                            device_id_type=pl.DeviceIdType.MESH)
    for d in range(1, n_col):
        pl.semaphore_signal(barrier, inc=1, device_id={"col": (me_c + d) % n_col},
                            device_id_type=pl.DeviceIdType.MESH)
    pl.semaphore_wait(barrier, n_row + n_col - 2)

    def share(peer, source):
        return remote(panels_ref.at[peer], whole.at[pl.ds(source * mine, mine)],
                      a_send.at[peer], a_recv.at[source], {"row": peer})

    for d in range(1, n_row):
        share((me_r + d) % n_row, me_r).start()
    whole[pl.ds(me_r * mine, mine)] = panels_ref[me_r]
    for cb in range(col_blocks):
        for rb in range(row_blocks):
            block = ainv_ref[rb * width:(rb + 1) * width, cb * width:(cb + 1) * width]
            high, low = split_bf16(block)
            high_ref[cb, rb] = high
            low_part_ref[cb, rb] = low
    for d in range(1, n_row):
        share(me_r, (me_r + d) % n_row).wait_recv()

    def pick(c):
        for s in range(col_live):
            place = c * col_live + s
            block = whole[order_ref[place]]
            spread[place] = jnp.where(live_ref[place] > 0, block, 0.0).T

    def ship(c, source):
        return remote(spread.at[pl.ds(c * col_live, col_live)], gathered.at[me_r, source],
                      c_send.at[c], c_recv.at[source], {"col": c})

    def pick_and_ship(c):
        pick(c)
        ship(c, me_c).start()

    def side_chip(t, side):
        chip = (1 - side) * (chips - 1 - t) + side * t
        active = jnp.where(side == 0, chip > z, chip < z)
        return chip, active

    pick(me_c)
    gathered[me_r, me_c] = spread[pl.ds(me_c * col_live, col_live)]

    def ship_step(i, carry):
        chip, active = side_chip(i // 2, i % 2)

        @pl.when(active)
        def _():
            pick_and_ship(2 * chip + core)
            pick_and_ship(2 * chip + 1 - core)

        return carry

    lax.fori_loop(0, 2 * chips, ship_step, 0)
    pick_and_ship(sibling)

    def pass_on(c, peer, source):
        return remote(gathered.at[source, c], gathered.at[source, c],
                      g_send.at[peer, c], g_recv.at[source, c], {"row": peer})

    def forward(c):
        for d in range(1, n_row):
            pass_on(c, (me_r + d) % n_row, me_r).start()

    forward(me_c)

    def forward_step(i, carry):
        chip, active = side_chip(i // 2, i % 2)

        @pl.when(active)
        def _():
            for c in (2 * chip + core, 2 * chip + 1 - core):
                ship(me_c, c).wait_recv()
                forward(c)

        return carry

    lax.fori_loop(0, 2 * chips, forward_step, 0)
    ship(me_c, sibling).wait_recv()
    forward(sibling)

    def local_copy(peer, source):
        return remote(spread.at[pl.ds(peer * row_live, row_live)], local.at[source],
                      l_send.at[peer], l_recv.at[source], {"row": peer})

    for d in range(1, n_row):
        local_copy((me_r + d) % n_row, me_r).start()
    local[me_r] = spread[pl.ds(me_r * row_live, row_live)]

    def product(c, chip, out):
        for d in range(1, n_row):
            pass_on(c, me_r, (me_r + d) % n_row).wait_recv()
        for node in range(per_col):
            rows = []
            for panel in range(2):
                for part in range(parts):
                    source = (panel * per_col + node) * parts + part
                    rows.append(jnp.concatenate([gathered[source, c, s] for s in range(col_live)], axis=1))
            left_high, left_low = split_bf16(jnp.concatenate(rows, axis=0))
            left_all = jnp.concatenate([left_high, left_high, left_low], axis=1)
            at = c * per_col + node
            cols = [col_ref[at, s] for s in range(col_live)]
            for rb in range(row_live):
                row = row_ref[at, rb]
                high = [high_ref[cb, row] for cb in cols]
                low = [low_part_ref[cb, row] for cb in cols]
                right = jnp.concatenate(high + low + high, axis=1)
                total = lax.dot_general(
                    left_all, right, (((1,), (1,)), ((), ())), preferred_element_type=jnp.float32
                )
                for panel in range(2):
                    out[chip, panel * per_col + node, :, rb * width:(rb + 1) * width] = (
                        -total[panel * width:(panel + 1) * width]
                    )

    def to_mate(chip):
        return remote(away.at[chip], mate.at[chip], s_send.at[chip], s_recv.at[chip], {"col": sibling})

    def both_products(chip):
        product(2 * chip + 1 - core, chip, away)
        to_mate(chip).start()
        product(2 * chip + core, chip, own)

    def onward(chip, s, side):
        slot = jnp.where((side == 1) & (z - 1 == chip), chips, chip)
        return remote(own.at[chip, s], line.at[slot, s], z_send.at[chip, s], z_recv.at[slot, s],
                      {"col": me_c + 2 - 4 * side})

    def arrived(slot, s):
        remote(own.at[0, s], line.at[slot, s], z_send.at[0, s], z_recv.at[slot, s],
               {"col": sibling}).wait_recv()

    def chunk_step(t, carry):
        def compute_side(side, inner):
            chip, active = side_chip(t, side)

            @pl.when(active)
            def _():
                both_products(chip)
                to_mate(chip).wait_recv()

            return inner

        def send_side(i, inner):
            s = i // 2
            side = i % 2
            chip, active = side_chip(t, side)

            @pl.when(active)
            def _():
                own[chip, s] = own[chip, s] + mate[chip, s]

                @pl.when(jnp.where(side == 0, z > 0, z < chips - 1))
                def _():
                    arrived(chip, s)
                    own[chip, s] = own[chip, s] + line[chip, s]

                onward(chip, s, side).start()

            return inner

        lax.fori_loop(0, 2, compute_side, 0)
        lax.fori_loop(0, 2 * combos, send_side, 0)
        return carry

    lax.fori_loop(0, chips, chunk_step, 0)
    both_products(z)
    to_mate(z).wait_recv()

    def last_step(s, carry):
        own[z, s] = own[z, s] + mate[z, s]

        @pl.when(z > 0)
        def _():
            arrived(z, s)
            own[z, s] = own[z, s] + line[z, s]

        @pl.when(z < chips - 1)
        def _():
            arrived(chips, s)
            own[z, s] = own[z, s] + line[chips, s]

        return carry

    lax.fori_loop(0, combos, last_step, 0)
    for d in range(1, n_row):
        local_copy(me_r, (me_r + d) % n_row).wait_recv()

    up_off_ref[...] = jnp.zeros_like(up_off_ref)
    low_off_ref[...] = jnp.zeros_like(low_off_ref)
    part_rows = width // n_row

    def full(combo, place):
        return jnp.concatenate([local[combo * parts + part, place] for part in range(parts)], axis=0)

    for node in range(per_col):
        sums = [jnp.zeros((width, width), jnp.float32)] * 3
        for place in range(row_live):
            span = slice(place * width, (place + 1) * width)
            upper = jnp.where(up_ref[node, place] > 0, own[z, node, :, span], 0.0)
            lower = own[z, per_col + node, :, span] - tn(parent_ref[node], upper)
            lower = jnp.where(low_ref[node, place] > 0, lower, 0.0)
            for block in range(row_blocks):
                here = at_ref[node, place] == block
                to = slice(block * width, (block + 1) * width)
                up_off_ref[node, :, to] = jnp.where(here, upper, up_off_ref[node, :, to])
                low_off_ref[node, :, to] = jnp.where(here, lower, low_off_ref[node, :, to])
            local_up = full(node, place)
            local_low = full(per_col + node, place)
            sums = [sums[0] + nt(local_up, upper), sums[1] + nt(upper, local_low),
                    sums[2] + nt(local_low, lower)]
        for kind in range(3):
            for j in range(n_row):
                terms[j, kind * per_col + node] = sums[kind][j * part_rows:(j + 1) * part_rows]

    def scatter(peer, source):
        return remote(terms.at[peer], landed.at[source], t_send.at[0, peer], t_recv.at[0, source],
                      {"row": peer})

    def spread_total(peer, source):
        return remote(totals.at[source], totals.at[source], t_send.at[1, peer], t_recv.at[1, source],
                      {"row": peer})

    for d in range(1, n_row):
        scatter((me_r + d) % n_row, me_r).start()
    landed[me_r] = terms[me_r]
    for d in range(1, n_row):
        scatter(me_r, (me_r + d) % n_row).wait_recv()
    total = landed[0]
    for j in range(1, n_row):
        total = total + landed[j]
    totals[me_r] = total
    for d in range(1, n_row):
        spread_total((me_r + d) % n_row, me_r).start()
    for d in range(1, n_row):
        spread_total(me_r, (me_r + d) % n_row).wait_recv()

    def summed(kind, node):
        return jnp.concatenate([totals[j, kind * per_col + node] for j in range(n_row)], axis=0)

    for node in range(per_col):
        parent = parent_ref[node]
        diag_up = updinv_ref[node] - summed(0, node)
        prow = -(nn(diag_up, parent) + summed(1, node))
        up_diag_ref[node] = diag_up
        prow_ref[node] = prow
        low_diag_ref[node] = lowdinv_ref[node] - tn(parent, prow) - summed(2, node)

    for d in range(1, n_row):
        peer = (me_r + d) % n_row
        share(peer, me_r).wait_send()
        local_copy(peer, me_r).wait_send()
        scatter(peer, me_r).wait_send()
        spread_total(peer, me_r).wait_send()
        for c in range(n_col):
            pass_on(c, peer, me_r).wait_send()
    for d in range(1, n_col):
        ship((me_c + d) % n_col, me_c).wait_send()
    for chip in range(chips):
        to_mate(chip).wait_send()

    def drain(i, carry):
        chip = i // combos

        @pl.when(chip != z)
        def _():
            onward(chip, i % combos, jnp.where(chip > z, 0, 1)).wait_send()

        return carry

    lax.fori_loop(0, chips * combos, drain, 0)


def body(
    n_row,
    n_col,
    ainv_top,
    block_owner,
    upper_list,
    upper_len,
    upper_panel,
    upper_dinv,
    lower_len,
    lower_panel,
    lower_parent,
    lower_dinv,
):
    width = upper_dinv.shape[-1]
    per_col = upper_dinv.shape[0]
    local_rows, local_cols = ainv_top.shape
    row_blocks = local_rows // width
    col_blocks = local_cols // width
    row_live = row_blocks // 2
    col_live = col_blocks // 2
    total = block_owner.shape[0]
    listed = upper_list.shape[1]
    mine = listed // n_row
    combos = 2 * per_col
    parts = n_row // combos
    piece = width // parts
    here = lax.axis_index("row")

    every = jnp.arange(total, dtype=jnp.int32)
    places = jnp.arange(listed, dtype=jnp.int32)
    slots = jnp.sum(
        jnp.where(upper_list[:, :, None] == every, block_owner[None, None, :], 0), axis=2
    )
    rank = jnp.sum((slots[:, None, :] < slots[:, :, None]).astype(jnp.int32), axis=2)
    hit = rank[:, :, None] == places[None, None, :]
    order = jnp.sum(jnp.where(hit, places[None, :, None], 0), axis=1)
    sorted_slots = jnp.sum(jnp.where(hit, slots[:, :, None], 0), axis=1)
    live_up = (order < upper_len[:, None]).astype(jnp.int32)
    live_low = (order < lower_len[:, None]).astype(jnp.int32)
    all_slots = lax.all_gather(sorted_slots, "col", axis=0, tiled=True)

    panels = jnp.concatenate([upper_panel, lower_panel], axis=0)
    panels = panels.reshape(combos, mine, width, parts, piece)
    panels = panels.transpose(0, 3, 1, 2, 4).reshape(n_row, mine, width, piece)
    combo = here // parts
    node = combo % per_col
    live_all = jnp.concatenate([live_up, live_low], axis=0)
    col_here = lax.axis_index("col")
    row_at = lax.dynamic_slice_in_dim(all_slots, here * row_live, row_live, 1) - here * row_blocks
    col_at = lax.dynamic_slice_in_dim(all_slots, col_here * col_live, col_live, 1) - col_here * col_blocks
    mine_at = lax.dynamic_slice_in_dim(sorted_slots, here * row_live, row_live, 1) - here * row_blocks
    mine_up = lax.dynamic_slice_in_dim(live_up, here * row_live, row_live, 1)
    mine_low = lax.dynamic_slice_in_dim(live_low, here * row_live, row_live, 1)
    chips = n_col // 2
    live_width = row_live * width
    f32 = jnp.float32
    dma = pltpu.SemaphoreType.DMA
    square = jax.ShapeDtypeStruct((per_col, width, width), f32)
    wide = jax.ShapeDtypeStruct((per_col, width, local_rows), f32)
    chunks = VMEM((chips, combos, width, live_width), f32)
    shares = VMEM((n_row, 3 * per_col, width // n_row, width), f32)
    return pl.pallas_call(
        functools.partial(mega_kernel, per_col, n_row, n_col),
        out_shape=(wide, square, wide, square, square),
        in_specs=[pl.BlockSpec(memory_space=SMEM)] * 7 + [pl.BlockSpec(memory_space=VMEM)] * 5,
        out_specs=(pl.BlockSpec(memory_space=VMEM),) * 5,
        scratch_shapes=[
            VMEM((listed, width, piece), f32),
            VMEM((listed, piece, width), f32),
            VMEM((n_row, n_col, col_live, piece, width), f32),
            VMEM((col_blocks, row_blocks, width, width), jnp.bfloat16),
            VMEM((col_blocks, row_blocks, width, width), jnp.bfloat16),
            chunks,
            chunks,
            chunks,
            VMEM((chips + 1, combos, width, live_width), f32),
            VMEM((n_row, row_live, piece, width), f32),
            shares,
            shares,
            shares,
            dma((n_row,)),
            dma((n_row,)),
            dma((n_col,)),
            dma((n_col,)),
            dma((n_row, n_col)),
            dma((n_row, n_col)),
            dma((n_row,)),
            dma((n_row,)),
            dma((chips,)),
            dma((chips,)),
            dma((chips, combos)),
            dma((chips + 1, combos)),
            dma((2, n_row)),
            dma((2, n_row)),
        ],
        compiler_params=pltpu.CompilerParams(
            collective_id=0, has_side_effects=True, vmem_limit_bytes=60 * 1024 * 1024
        ),
        name="selected_inverse",
    )(
        order[node], live_all[combo], row_at, col_at, mine_at, mine_up, mine_low,
        panels, ainv_top, lower_parent, upper_dinv, lower_dinv,
    )


def solution(mesh):
    in_specs = (
        P("row", "col"),
        P(),
        P("col", None),
        P("col"),
        P("col", "row", None),
        P("col", None, None),
        P("col"),
        P("col", "row", None),
        P("col", None, None),
        P("col", None, None),
    )
    out_specs = (
        P("col", None, "row"),
        P("col", None, None),
        P("col", None, "row"),
        P("col", None, None),
        P("col", None, None),
    )
    inner = functools.partial(body, mesh.shape["row"], mesh.shape["col"])
    return jax.shard_map(inner, mesh=mesh, in_specs=in_specs, out_specs=out_specs, check_vma=False)
```

time: 276 us -> 184 us (0.67)
  waiting for transfers between devices: 185 us -> 0 us
  Pallas kernels: 17.8 us -> 161 us
  blocking collectives: 38.3 us -> 9.04 us
  between operations: 13.9 us -> 0.7 us
  starting transfers between devices: 7.59 us -> 0 us
  matrix products: 3.22 us -> 0 us
  local copies, waits for them, and re-layouts: 3.56 us -> 6.61 us
    pallas_call x3 -> x1, Pallas kernels: 17.8 us -> 161 us  [body(): pl.pallas_call(functools.partial(mega_kernel, per_col, n_row, n_col), out...]
    reduce_scatter x1 -> x0, waiting for transfers between devices: 69.6 us -> none  [body(): sums = lax.psum_scatter(partial, 'col', scatter_dimension=0, tiled=True)[0]]
    psum x1 -> x0, waiting for transfers between devices: 45.1 us -> none  [body(): totals = lax.psum(terms, 'row')]
    all_gather x1 -> x0, waiting for transfers between devices: 43.7 us -> none  [body(): gathered = lax.all_gather(landed, 'row', axis=0, tiled=False)]
    all_to_all x1 -> x0, blocking collectives: 28.6 us -> none  [body(): lax.all_to_all(spread.reshape(n_col, col_live, piece, width), 'col', spli...]
    all_to_all x2 -> x0, waiting for transfers between devices: 26.7 us -> none  [the longest x1 13.7 us: body(): lax.all_to_all(spread.reshape(n_row, row_live, piece, width), 'row', spli...]
    all_to_all x2 -> x0, starting transfers between devices: 7.51 us -> none  [the longest x1 3.85 us: body(): lax.all_to_all(panels, 'row', split_axis=0, concat_axis=0, tiled=True)]
    dot_general x2 -> x0, matrix products: 3.22 us -> none  [the longest x1 2 us: body(): jnp.einsum('bji,bjk->bik', lower_parent, parent_row, precision=highest)]
  transfers between devices with their start and end apart: 5 -> 0, of which waited for: 5 -> 0; matrix products, arithmetic and copies ran while one was open for 0% -> 0% of each run, Pallas kernels for 0% -> 0%
where the time goes in v2:
time: 184 us; the launch traced here: 183 us
  Pallas kernels  161 us (88%)
  blocking collectives  9.04 us (5%)
  local copies, waits for them, and re-layouts  6.61 us (4%)
  other arithmetic  6.13 us (3%)
    pallas_call x1, Pallas kernels, body(): pl.pallas_call(functools.partial(mega_kernel, per_col, n_row, n_col), out...  161 us
    all_gather x1, blocking collectives, body(): all_slots = lax.all_gather(sorted_slots, 'col', axis=0, tiled=True)  9.04 us
    unnamed x13, local copies, waits for them, and re-layouts  5.37 us

profile of v2, /device:TPU:16, one launch (start us, length us, event | category | flops | bytes accessed | tf_op | source)
XLA Modules:
  0.0 183.5 jit_solution(12848439075420129530)
XLA Ops:
  0.6 0.9 select_reduce_fusion.2
  1.5 0.2 convert_reduce_fusion
  1.7 0.1 select_reduce_fusion
  1.8 0.6 fusion.at_ref
  2.5 0.7 compare_convert_fusion.1
  3.2 0.6 fusion.1
  3.8 0.6 constant_dynamic-slice_fusion
  4.5 9.0 %all-gather = s32[8,2,16]{2,1,0:T(2,128)S(1)} all-gather(s32[1,2,16]{2,1,0:T(2,128)S(1)} %bitcast.10), channel_id=1, replica_groups=mesh['row'=4,'col'=8] {'col'}, dimensions={0}, use_global_device_ids=true | all-gather | bytes 1152 | tf_op jit(solution)/shard_map/all_gather | solution.py:384
  13.5 0.7 dynamic-slice_subtract_fusion.col_ref
  14.2 0.7 dynamic-slice_subtract_fusion.1.row_ref
  14.8 2.2 %pad_maximum_fusion = f32[4,512,128]{2,1,0:T(8,128)} fusion(f32[2,512,128]{2,1,0:T(8,128)} %param.17, f32[2,512,128]{2,1,0:T(8,128)} %param.14), kind=kLoop, calls=%fused_computation | loop fusion | flops 262144 | bytes 2097152 | tf_op jit(solution)/shard_map/concatenate | solution.py:386
  17.1 161.0 %selected_inverse.1 = (f32[2,128,1024]{2,1,0:T(8,128)}, f32[2,128,128]{2,1,0:T(8,128)}, f32[2,128,1024]{2,1,0:T(8,128)}, f32[2,128,128]{2,1,0:T(8,128)}, f32[2,128,128]{2,1,0:T(8,128)}) custom-call(s32[16]{0:T(128)} %get-tuple-element.11.order_ref, s32[16]{0:T(128)} %get-tuple-element.12.live_ref, s32[16,4]{1,0:T(8,128)} %dynamic-slice_subtract_fusion.1.row_ref, ...), custom_call_target="tpu_custom_call" | custom-call | tf_op jit(solution)/shard_map/selected_inverse/pallas_call | solution.py:406
  178.1 0.0 copy-start.3
  178.1 0.0 copy-start
  178.1 0.0 copy-start.2
  178.1 0.0 copy-start.1
  178.1 2.4 %copy.20 = f32[2,128,1024]{2,1,0:T(8,128)} copy(f32[2,128,1024]{2,1,0:T(8,128)} %get-tuple-element.18) | data formatting | bytes 2097152
  180.5 0.0 copy-done.3
  180.5 0.7 copy.21
  181.2 0.0 copy-done
  181.2 1.0 copy.22
  182.1 0.0 copy-done.2
  182.1 0.7 copy.23
  182.8 0.0 copy-done.1
  182.8 0.7 copy.24
  (1 shorter events, 0.0 us)
Async XLA Ops:
  178.1 2.5 %copy-start.3 = (f32[2,128,128]{2,1,0:T(8,128)S(1)}, f32[2,128,128]{2,1,0:T(8,128)}, u32[]{:S(2)}) copy-start(f32[2,128,128]{2,1,0:T(8,128)} %get-tuple-element.19) | copy-start | bytes 393220
  178.1 3.1 %copy-start = (f32[2,128,1024]{2,1,0:T(8,128)S(1)}, f32[2,128,1024]{2,1,0:T(8,128)}, u32[]{:S(2)}) copy-start(f32[2,128,1024]{2,1,0:T(8,128)} %get-tuple-element.20) | copy-start | bytes 3145732
  178.1 4.1 %copy-start.2 = (f32[2,128,128]{2,1,0:T(8,128)S(1)}, f32[2,128,128]{2,1,0:T(8,128)}, u32[]{:S(2)}) copy-start(f32[2,128,128]{2,1,0:T(8,128)} %get-tuple-element.21) | copy-start | bytes 393220
  178.1 4.7 %copy-start.1 = (f32[2,128,128]{2,1,0:T(8,128)S(1)}, f32[2,128,128]{2,1,0:T(8,128)}, u32[]{:S(2)}) copy-start(f32[2,128,128]{2,1,0:T(8,128)} %get-tuple-element.22) | copy-start | bytes 393220

commit v3 on v2

--- a/solution.py
+++ b/solution.py
@@ -37,14 +37,17 @@
 
 
 def mega_kernel(
-    per_col, n_row, n_col,
-    order_ref, live_ref, row_ref, col_ref, at_ref, up_ref, low_ref,
-    panels_ref, ainv_ref, parent_ref, updinv_ref, lowdinv_ref,
-    up_off_ref, up_diag_ref, low_off_ref, prow_ref, low_diag_ref,
-    whole, spread, gathered, high_ref, low_part_ref, own, away, mate, line, local, terms, landed, totals,
-    a_send, a_recv, c_send, c_recv, g_send, g_recv, l_send, l_recv,
-    s_send, s_recv, z_send, z_recv, t_send, t_recv,
+    per_col, n_row, n_col, n_panels,
+    order_ref, up_len_ref, low_len_ref, tile_ref, *refs,
 ):
+    panel_refs, refs = refs[:n_panels], refs[n_panels:]
+    (
+        ainv_hbm, parent_ref, up_ref, low_ref, totals_ref,
+        whole, spread, gathered, ainv_ref, high_ref, low_part_ref, own, away, mate, line, local,
+        terms, landed, totals, tiles, slots,
+        a_send, a_recv, c_send, c_recv, g_send, g_recv, l_send, l_recv,
+        s_send, s_recv, z_send, z_recv, t_send, t_recv, q_send, q_recv, own_sem, ainv_sem, slot_sem,
+    ) = refs
     me_r = lax.axis_index("row")
     me_c = lax.axis_index("col")
     chips = n_col // 2
@@ -53,7 +56,7 @@
     sibling = me_c + 1 - 2 * core
     combos = 2 * per_col
     parts = n_row // combos
-    mine = panels_ref.shape[1]
+    mine = panel_refs[0].shape[1]
     col_blocks, row_blocks, width, _ = high_ref.shape
     col_live = gathered.shape[2]
     row_live = local.shape[1]
@@ -73,27 +76,57 @@
                             device_id_type=pl.DeviceIdType.MESH)
     pl.semaphore_wait(barrier, n_row + n_col - 2)
 
+    def held(peer):
+        if n_panels == 1:
+            return panel_refs[0].at[peer]
+        return panel_refs[peer // per_col].at[peer % per_col]
+
     def share(peer, source):
-        return remote(panels_ref.at[peer], whole.at[pl.ds(source * mine, mine)],
+        return remote(held(peer), whole.at[pl.ds(source * mine, mine)],
                       a_send.at[peer], a_recv.at[source], {"row": peer})
 
-    for d in range(1, n_row):
-        share((me_r + d) % n_row, me_r).start()
-    whole[pl.ds(me_r * mine, mine)] = panels_ref[me_r]
+    def keep(peer):
+        return pltpu.make_async_copy(held(peer), whole.at[pl.ds(me_r * mine, mine)], own_sem)
+
+    def each_peer(act):
+        for peer in range(n_row):
+            @pl.when(peer != me_r)
+            def _():
+                act(share(peer, me_r))
+
+    def slot_copy(c, source):
+        return remote(tile_ref, tiles.at[source], q_send.at[c], q_recv.at[source], {"col": c})
+
+    each_peer(lambda copy: copy.start())
+    for peer in range(n_row):
+        @pl.when(peer == me_r)
+        def _():
+            keep(peer).start()
+    fetch = pltpu.make_async_copy(ainv_hbm, ainv_ref, ainv_sem)
+    fetch.start()
+    for d in range(1, n_col):
+        slot_copy((me_c + d) % n_col, me_c).start()
+    tiles[me_c] = tile_ref[...]
+    fetch.wait()
     for cb in range(col_blocks):
         for rb in range(row_blocks):
             block = ainv_ref[rb * width:(rb + 1) * width, cb * width:(cb + 1) * width]
             high, low = split_bf16(block)
             high_ref[cb, rb] = high
             low_part_ref[cb, rb] = low
+    keep(0).wait()
     for d in range(1, n_row):
-        share(me_r, (me_r + d) % n_row).wait_recv()
+        share(0, (me_r + d) % n_row).wait_recv()
+
+    my_combo = me_r // parts
+    my_node = my_combo % per_col
+    my_len = jnp.where(my_combo < per_col, up_len_ref[my_node], low_len_ref[my_node])
 
     def pick(c):
         for s in range(col_live):
             place = c * col_live + s
-            block = whole[order_ref[place]]
-            spread[place] = jnp.where(live_ref[place] > 0, block, 0.0).T
+            listed_at = order_ref[my_node, place]
+            spread[place] = jnp.where(listed_at < my_len, whole[listed_at], 0.0).T
 
     def ship(c, source):
         return remote(spread.at[pl.ds(c * col_live, col_live)], gathered.at[me_r, source],
@@ -133,8 +166,10 @@
             pass_on(c, (me_r + d) % n_row, me_r).start()
 
     forward(me_c)
-
-    def forward_step(i, carry):
+    ship(me_c, sibling).wait_recv()
+    forward(sibling)
+
+    def forward_side(i, carry):
         chip, active = side_chip(i // 2, i % 2)
 
         @pl.when(active)
@@ -145,9 +180,7 @@
 
         return carry
 
-    lax.fori_loop(0, 2 * chips, forward_step, 0)
-    ship(me_c, sibling).wait_recv()
-    forward(sibling)
+    lax.fori_loop(0, 4, forward_side, 0)
 
     def local_copy(peer, source):
         return remote(spread.at[pl.ds(peer * row_live, row_live)], local.at[source],
@@ -156,6 +189,12 @@
     for d in range(1, n_row):
         local_copy((me_r + d) % n_row, me_r).start()
     local[me_r] = spread[pl.ds(me_r * row_live, row_live)]
+
+    for d in range(1, n_col):
+        slot_copy(me_c, (me_c + d) % n_col).wait_recv()
+    to_scalars = pltpu.make_async_copy(tiles, slots, slot_sem)
+    to_scalars.start()
+    to_scalars.wait()
 
     def product(c, chip, out):
         for d in range(1, n_row):
@@ -168,10 +207,9 @@
                     rows.append(jnp.concatenate([gathered[source, c, s] for s in range(col_live)], axis=1))
             left_high, left_low = split_bf16(jnp.concatenate(rows, axis=0))
             left_all = jnp.concatenate([left_high, left_high, left_low], axis=1)
-            at = c * per_col + node
-            cols = [col_ref[at, s] for s in range(col_live)]
+            cols = [lax.rem(slots[c, node, me_c * col_live + s], col_blocks) for s in range(col_live)]
             for rb in range(row_live):
-                row = row_ref[at, rb]
+                row = lax.rem(slots[c, node, me_r * row_live + rb], row_blocks)
                 high = [high_ref[cb, row] for cb in cols]
                 low = [low_part_ref[cb, row] for cb in cols]
                 right = jnp.concatenate(high + low + high, axis=1)
@@ -231,6 +269,7 @@
 
         lax.fori_loop(0, 2, compute_side, 0)
         lax.fori_loop(0, 2 * combos, send_side, 0)
+        lax.fori_loop(2 * t + 4, 2 * t + 6, forward_side, 0)
         return carry
 
     lax.fori_loop(0, chips, chunk_step, 0)
@@ -252,93 +291,133 @@
 
         return carry
 
-    lax.fori_loop(0, combos, last_step, 0)
+    part_rows = width // n_row
+    rounds = ((0, 2 * per_col), (2 * per_col, per_col))
+
+    def full(combo, place):
+        return jnp.concatenate([local[combo * parts + part, place] for part in range(parts)], axis=0)
+
+    def spans():
+        return [(place, slice(place * width, (place + 1) * width)) for place in range(row_live)]
+
+    def live(node, place, length_ref):
+        return order_ref[node, me_r * row_live + place] < length_ref[node]
+
+    def put(kind, node, value):
+        for j in range(n_row):
+            terms[j, kind * per_col + node] = value[j * part_rows:(j + 1) * part_rows]
+
+    def scatter(at, peer, source):
+        part = pl.ds(*rounds[at])
+        return remote(terms.at[peer, part], landed.at[source, part], t_send.at[at, peer],
+                      t_recv.at[at, source], {"row": peer})
+
+    def spread_total(at, peer, source):
+        part = pl.ds(*rounds[at])
+        return remote(totals.at[source, part], totals.at[source, part], t_send.at[2 + at, peer],
+                      t_recv.at[2 + at, source], {"row": peer})
+
+    def start_round(at):
+        for d in range(1, n_row):
+            scatter(at, (me_r + d) % n_row, me_r).start()
+        part = pl.ds(*rounds[at])
+        landed[me_r, part] = terms[me_r, part]
+
+    def sum_round(at):
+        for d in range(1, n_row):
+            scatter(at, me_r, (me_r + d) % n_row).wait_recv()
+        part = pl.ds(*rounds[at])
+        total = landed[0, part]
+        for j in range(1, n_row):
+            total = total + landed[j, part]
+        totals[me_r, part] = total
+        for d in range(1, n_row):
+            spread_total(at, (me_r + d) % n_row, me_r).start()
+
     for d in range(1, n_row):
         local_copy(me_r, (me_r + d) % n_row).wait_recv()
-
+    lax.fori_loop(0, per_col, last_step, 0)
+    for node in range(per_col):
+        upper_term = jnp.zeros((width, width), jnp.float32)
+        cross_term = jnp.zeros((width, width), jnp.float32)
+        for place, span in spans():
+            upper = jnp.where(live(node, place, up_len_ref), own[z, node, :, span], 0.0)
+            up_ref[node, :, span] = upper
+            upper_term = upper_term + nt(full(node, place), upper)
+            cross_term = cross_term + nt(upper, full(per_col + node, place))
+        put(0, node, upper_term)
+        put(1, node, cross_term)
+    start_round(0)
+    for node in range(per_col):
+        low_ref[node] = tn(parent_ref[node], up_ref[node])
+    lax.fori_loop(per_col, combos, last_step, 0)
+    for node in range(per_col):
+        lower_term = jnp.zeros((width, width), jnp.float32)
+        for place, span in spans():
+            lower = own[z, per_col + node, :, span] - low_ref[node, :, span]
+            lower = jnp.where(live(node, place, low_len_ref), lower, 0.0)
+            low_ref[node, :, span] = lower
+            lower_term = lower_term + nt(full(per_col + node, place), lower)
+        put(2, node, lower_term)
+    start_round(1)
+    sum_round(0)
+    sum_round(1)
+    for at in range(2):
+        for d in range(1, n_row):
+            spread_total(at, me_r, (me_r + d) % n_row).wait_recv()
+    totals_ref[...] = totals[...]
+
+    for d in range(1, n_row):
+        peer = (me_r + d) % n_row
+        local_copy(peer, me_r).wait_send()
+        for at in range(2):
+            scatter(at, peer, me_r).wait_send()
+            spread_total(at, peer, me_r).wait_send()
+        for c in range(n_col):
+            pass_on(c, peer, me_r).wait_send()
+    for d in range(1, n_col):
+        ship((me_c + d) % n_col, me_c).wait_send()
+        slot_copy((me_c + d) % n_col, me_c).wait_send()
+    each_peer(lambda copy: copy.wait_send())
+    for chip in range(chips):
+        to_mate(chip).wait_send()
+
+    def drain(i, carry):
+        chip = i // combos
+
+        @pl.when(chip != z)
+        def _():
+            onward(chip, i % combos, jnp.where(chip > z, 0, 1)).wait_send()
+
+        return carry
+
+    lax.fori_loop(0, chips * combos, drain, 0)
+
+
+def write_kernel(row_blocks, slot_ref, up_ref, low_ref, totals_ref, parent_ref, updinv_ref, lowdinv_ref,
+                 up_off_ref, up_diag_ref, low_off_ref, prow_ref, low_diag_ref):
+    per_col, width, _ = parent_ref.shape
+    n_row = totals_ref.shape[0]
+    row_live = up_ref.shape[2] // width
     up_off_ref[...] = jnp.zeros_like(up_off_ref)
     low_off_ref[...] = jnp.zeros_like(low_off_ref)
-    part_rows = width // n_row
-
-    def full(combo, place):
-        return jnp.concatenate([local[combo * parts + part, place] for part in range(parts)], axis=0)
+
+    def summed(kind, node):
+        return jnp.concatenate([totals_ref[j, kind * per_col + node] for j in range(n_row)], axis=0)
 
     for node in range(per_col):
-        sums = [jnp.zeros((width, width), jnp.float32)] * 3
         for place in range(row_live):
             span = slice(place * width, (place + 1) * width)
-            upper = jnp.where(up_ref[node, place] > 0, own[z, node, :, span], 0.0)
-            lower = own[z, per_col + node, :, span] - tn(parent_ref[node], upper)
-            lower = jnp.where(low_ref[node, place] > 0, lower, 0.0)
-            for block in range(row_blocks):
-                here = at_ref[node, place] == block
-                to = slice(block * width, (block + 1) * width)
-                up_off_ref[node, :, to] = jnp.where(here, upper, up_off_ref[node, :, to])
-                low_off_ref[node, :, to] = jnp.where(here, lower, low_off_ref[node, :, to])
-            local_up = full(node, place)
-            local_low = full(per_col + node, place)
-            sums = [sums[0] + nt(local_up, upper), sums[1] + nt(upper, local_low),
-                    sums[2] + nt(local_low, lower)]
-        for kind in range(3):
-            for j in range(n_row):
-                terms[j, kind * per_col + node] = sums[kind][j * part_rows:(j + 1) * part_rows]
-
-    def scatter(peer, source):
-        return remote(terms.at[peer], landed.at[source], t_send.at[0, peer], t_recv.at[0, source],
-                      {"row": peer})
-
-    def spread_total(peer, source):
-        return remote(totals.at[source], totals.at[source], t_send.at[1, peer], t_recv.at[1, source],
-                      {"row": peer})
-
-    for d in range(1, n_row):
-        scatter((me_r + d) % n_row, me_r).start()
-    landed[me_r] = terms[me_r]
-    for d in range(1, n_row):
-        scatter(me_r, (me_r + d) % n_row).wait_recv()
-    total = landed[0]
-    for j in range(1, n_row):
-        total = total + landed[j]
-    totals[me_r] = total
-    for d in range(1, n_row):
-        spread_total((me_r + d) % n_row, me_r).start()
-    for d in range(1, n_row):
-        spread_total(me_r, (me_r + d) % n_row).wait_recv()
-
-    def summed(kind, node):
-        return jnp.concatenate([totals[j, kind * per_col + node] for j in range(n_row)], axis=0)
-
-    for node in range(per_col):
+            block = lax.rem(slot_ref[node, lax.axis_index("row") * row_live + place], row_blocks)
+            at = pl.ds(pl.multiple_of(block * width, width), width)
+            up_off_ref[node, :, at] = up_ref[node, :, span]
+            low_off_ref[node, :, at] = low_ref[node, :, span]
         parent = parent_ref[node]
         diag_up = updinv_ref[node] - summed(0, node)
         prow = -(nn(diag_up, parent) + summed(1, node))
         up_diag_ref[node] = diag_up
         prow_ref[node] = prow
         low_diag_ref[node] = lowdinv_ref[node] - tn(parent, prow) - summed(2, node)
-
-    for d in range(1, n_row):
-        peer = (me_r + d) % n_row
-        share(peer, me_r).wait_send()
-        local_copy(peer, me_r).wait_send()
-        scatter(peer, me_r).wait_send()
-        spread_total(peer, me_r).wait_send()
-        for c in range(n_col):
-            pass_on(c, peer, me_r).wait_send()
-    for d in range(1, n_col):
-        ship((me_c + d) % n_col, me_c).wait_send()
-    for chip in range(chips):
-        to_mate(chip).wait_send()
-
-    def drain(i, carry):
-        chip = i // combos
-
-        @pl.when(chip != z)
-        def _():
-            onward(chip, i % combos, jnp.where(chip > z, 0, 1)).wait_send()
-
-        return carry
-
-    lax.fori_loop(0, chips * combos, drain, 0)
 
 
 def body(
@@ -368,7 +447,6 @@
     combos = 2 * per_col
     parts = n_row // combos
     piece = width // parts
-    here = lax.axis_index("row")
 
     every = jnp.arange(total, dtype=jnp.int32)
     places = jnp.arange(listed, dtype=jnp.int32)
@@ -379,22 +457,14 @@
     hit = rank[:, :, None] == places[None, None, :]
     order = jnp.sum(jnp.where(hit, places[None, :, None], 0), axis=1)
     sorted_slots = jnp.sum(jnp.where(hit, slots[:, :, None], 0), axis=1)
-    live_up = (order < upper_len[:, None]).astype(jnp.int32)
-    live_low = (order < lower_len[:, None]).astype(jnp.int32)
-    all_slots = lax.all_gather(sorted_slots, "col", axis=0, tiled=True)
-
-    panels = jnp.concatenate([upper_panel, lower_panel], axis=0)
-    panels = panels.reshape(combos, mine, width, parts, piece)
-    panels = panels.transpose(0, 3, 1, 2, 4).reshape(n_row, mine, width, piece)
-    combo = here // parts
-    node = combo % per_col
-    live_all = jnp.concatenate([live_up, live_low], axis=0)
-    col_here = lax.axis_index("col")
-    row_at = lax.dynamic_slice_in_dim(all_slots, here * row_live, row_live, 1) - here * row_blocks
-    col_at = lax.dynamic_slice_in_dim(all_slots, col_here * col_live, col_live, 1) - col_here * col_blocks
-    mine_at = lax.dynamic_slice_in_dim(sorted_slots, here * row_live, row_live, 1) - here * row_blocks
-    mine_up = lax.dynamic_slice_in_dim(live_up, here * row_live, row_live, 1)
-    mine_low = lax.dynamic_slice_in_dim(live_low, here * row_live, row_live, 1)
+    tile = jnp.pad(sorted_slots, ((0, 8 - per_col), (0, 128 - listed)))
+
+    if parts == 1:
+        panels = tuple(panel.reshape(per_col, mine, width, width) for panel in (upper_panel, lower_panel))
+    else:
+        both = jnp.concatenate([upper_panel, lower_panel], axis=0)
+        both = both.reshape(combos, mine, width, parts, piece)
+        panels = (both.transpose(0, 3, 1, 2, 4).reshape(n_row, mine, width, piece),)
     chips = n_col // 2
     live_width = row_live * width
     f32 = jnp.float32
@@ -403,15 +473,22 @@
     wide = jax.ShapeDtypeStruct((per_col, width, local_rows), f32)
     chunks = VMEM((chips, combos, width, live_width), f32)
     shares = VMEM((n_row, 3 * per_col, width // n_row, width), f32)
-    return pl.pallas_call(
-        functools.partial(mega_kernel, per_col, n_row, n_col),
-        out_shape=(wide, square, wide, square, square),
-        in_specs=[pl.BlockSpec(memory_space=SMEM)] * 7 + [pl.BlockSpec(memory_space=VMEM)] * 5,
-        out_specs=(pl.BlockSpec(memory_space=VMEM),) * 5,
+    rows = jax.ShapeDtypeStruct((per_col, width, live_width), f32)
+    upper_rows, lower_rows, totals = pl.pallas_call(
+        functools.partial(mega_kernel, per_col, n_row, n_col, len(panels)),
+        out_shape=(rows, rows, jax.ShapeDtypeStruct((n_row, 3 * per_col, width // n_row, width), f32)),
+        in_specs=(
+            [pl.BlockSpec(memory_space=SMEM)] * 3
+            + [pl.BlockSpec(memory_space=VMEM)]
+            + [pl.BlockSpec(memory_space=pl.ANY)] * (len(panels) + 1)
+            + [pl.BlockSpec(memory_space=VMEM)]
+        ),
+        out_specs=(pl.BlockSpec(memory_space=VMEM),) * 3,
         scratch_shapes=[
             VMEM((listed, width, piece), f32),
             VMEM((listed, piece, width), f32),
             VMEM((n_row, n_col, col_live, piece, width), f32),
+            VMEM((local_rows, local_cols), f32),
             VMEM((col_blocks, row_blocks, width, width), jnp.bfloat16),
             VMEM((col_blocks, row_blocks, width, width), jnp.bfloat16),
             chunks,
@@ -422,6 +499,8 @@
             shares,
             shares,
             shares,
+            VMEM((n_col, 8, 128), jnp.int32),
+            SMEM((n_col, 8, 128), jnp.int32),
             dma((n_row,)),
             dma((n_row,)),
             dma((n_col,)),
@@ -434,17 +513,27 @@
             dma((chips,)),
             dma((chips, combos)),
             dma((chips + 1, combos)),
-            dma((2, n_row)),
-            dma((2, n_row)),
+            dma((4, n_row)),
+            dma((4, n_row)),
+            dma((n_col,)),
+            dma((n_col,)),
+            dma(()),
+            dma(()),
+            dma(()),
         ],
         compiler_params=pltpu.CompilerParams(
             collective_id=0, has_side_effects=True, vmem_limit_bytes=60 * 1024 * 1024
         ),
         name="selected_inverse",
-    )(
-        order[node], live_all[combo], row_at, col_at, mine_at, mine_up, mine_low,
-        panels, ainv_top, lower_parent, upper_dinv, lower_dinv,
-    )
+    )(order, upper_len, lower_len, tile, *panels, ainv_top, lower_parent)
+    return pl.pallas_call(
+        functools.partial(write_kernel, row_blocks),
+        out_shape=(wide, square, wide, square, square),
+        in_specs=[pl.BlockSpec(memory_space=SMEM)] + [pl.BlockSpec(memory_space=VMEM)] * 6,
+        out_specs=(pl.BlockSpec(memory_space=VMEM),) * 5,
+        compiler_params=pltpu.CompilerParams(vmem_limit_bytes=32 * 1024 * 1024),
+        name="write_out",
+    )(sorted_slots, upper_rows, lower_rows, totals, lower_parent, upper_dinv, lower_dinv)
 
 
 def solution(mesh):

time: 184 us -> 160 us (0.87)
  blocking collectives: 9.04 us -> 0 us
  Pallas kernels: 161 us -> 154 us
  other arithmetic: 6.13 us -> 1.77 us
  local copies, waits for them, and re-layouts: 6.61 us -> 3.68 us
    all_gather x1 -> x0, blocking collectives: 9.04 us -> none  [body(): all_slots = lax.all_gather(sorted_slots, 'col', axis=0, tiled=True)]
    pallas_call x1 -> x2, Pallas kernels: 161 us -> 154 us  [the longest x1 151 us: body(): pl.pallas_call(functools.partial(mega_kernel, per_col, n_row, n_col, len(...]
    unnamed x13 -> x12, local copies, waits for them, and re-layouts: 5.37 us -> 3.09 us
    concatenate x2 -> x0, other arithmetic: 2.25 us -> none  [the longest x1 2.24 us: body(): panels = jnp.concatenate([upper_panel, lower_panel], axis=0)]
    sub x3 -> x0, other arithmetic: 1.99 us -> none  [the longest x1 0.67 us: body(): lax.dynamic_slice_in_dim(all_slots, col_here * col_live, col_live, 1)]
where the time goes in v3:
time: 160 us
  Pallas kernels  154 us (96%)
  local copies, waits for them, and re-layouts  3.68 us (2%)
  other arithmetic  1.77 us (1%)
    pallas_call x1, Pallas kernels, body(): pl.pallas_call(functools.partial(mega_kernel, per_col, n_row, n_col, len(...  151 us

profile of v3, /device:TPU:16, one launch (start us, length us, event | category | flops | bytes accessed | tf_op | source)
XLA Modules:
  0.0 159.9 jit_solution(10977189517387200630)
XLA Ops:
  0.6 0.0 copy-start.2
  0.6 0.0 copy-start.5
  0.7 0.0 copy-start.4
  0.7 0.9 select_reduce_fusion.2
  1.6 0.2 convert_reduce_fusion
  1.8 0.7 select_reduce_fusion
  2.4 0.6 pad.4.tile_ref
  3.0 151.2 %selected_inverse.1 = (f32[2,128,512]{2,1,0:T(8,128)}, f32[2,128,512]{2,1,0:T(8,128)}, f32[4,6,32,128]{3,2,1,0:T(8,128)}) custom-call(s32[2,16]{1,0:T(2,128)} %get-tuple-element.11.order_ref, s32[2]{0:T(128)} %up_len_ref.1, s32[2]{0:T(128)} %low_len_ref.1, s32[8,128]{1,0:T(8,128)} %pad.4.tile_ref, f32[2,4,128,128]{3,2,1,0:T(8,128)} %bitcast.2, ...), custom_call_target="tpu_custom_call" | custom-call | tf_op jit(solution)/shard_map/selected_inverse/pallas_call | solution.py:477
  154.2 0.0 copy-done.2
  154.2 0.0 copy-done.5
  154.2 0.0 copy-done.4
  154.2 0.0 copy-start
  154.2 1.0 copy-done
  155.3 0.0 copy-start.1
  155.3 1.0 copy-done.1
  156.3 0.0 copy-start.3
  156.3 1.0 copy-done.3
  157.3 2.6 %write_out.1 = (f32[2,128,1024]{2,1,0:T(8,128)}, f32[2,128,128]{2,1,0:T(8,128)}, f32[2,128,1024]{2,1,0:T(8,128)}, f32[2,128,128]{2,1,0:T(8,128)}, f32[2,128,128]{2,1,0:T(8,128)}) custom-call(s32[2,16]{1,0:T(2,128)S(1)} %get-tuple-element.12.slot_ref, f32[2,128,512]{2,1,0:T(8,128)S(1)} %copy-done, f32[2,128,512]{2,1,0:T(8,128)S(1)} %copy-done.1, ...), custom_call_target="tpu_custom_call" | custom-call | tf_op jit(solution)/shard_map/write_out/pallas_call | solution.py:529
Async XLA Ops:
  0.6 153.6 %copy-start.2 = (f32[2,128,128]{2,1,0:T(8,128)S(1)}, f32[2,128,128]{2,1,0:T(8,128)}, u32[]{:S(2)}) copy-start(f32[2,128,128]{2,1,0:T(8,128)} %parent_ref.1) | copy-start | bytes 393220
  0.6 153.6 %copy-start.5 = (f32[2,128,128]{2,1,0:T(8,128)S(1)}, f32[2,128,128]{2,1,0:T(8,128)}, u32[]{:S(2)}) copy-start(f32[2,128,128]{2,1,0:T(8,128)} %lowdinv_ref.1) | copy-start | bytes 393220
  0.7 153.6 %copy-start.4 = (f32[2,128,128]{2,1,0:T(8,128)S(1)}, f32[2,128,128]{2,1,0:T(8,128)}, u32[]{:S(2)}) copy-start(f32[2,128,128]{2,1,0:T(8,128)} %updinv_ref.1) | copy-start | bytes 393220
  154.2 1.0 copy-start
  155.3 1.0 copy-start.1
  156.3 1.0 copy-start.3

commit v4 on v3

--- a/solution.py
+++ b/solution.py
@@ -196,7 +196,7 @@
     to_scalars.start()
     to_scalars.wait()
 
-    def product(c, chip, out):
+    def product(c, chip, out, send=None):
         for d in range(1, n_row):
             pass_on(c, me_r, (me_r + d) % n_row).wait_recv()
         for node in range(per_col):
@@ -220,13 +220,16 @@
                     out[chip, panel * per_col + node, :, rb * width:(rb + 1) * width] = (
                         -total[panel * width:(panel + 1) * width]
                     )
-
-    def to_mate(chip):
-        return remote(away.at[chip], mate.at[chip], s_send.at[chip], s_recv.at[chip], {"col": sibling})
+            if send is not None:
+                for panel in range(2):
+                    send(chip, panel * per_col + node).start()
+
+    def to_mate(chip, s):
+        return remote(away.at[chip, s], mate.at[chip, s], s_send.at[chip, s], s_recv.at[chip, s],
+                      {"col": sibling})
 
     def both_products(chip):
-        product(2 * chip + 1 - core, chip, away)
-        to_mate(chip).start()
+        product(2 * chip + 1 - core, chip, away, to_mate)
         product(2 * chip + core, chip, own)
 
     def onward(chip, s, side):
@@ -245,7 +248,6 @@
             @pl.when(active)
             def _():
                 both_products(chip)
-                to_mate(chip).wait_recv()
 
             return inner
 
@@ -256,6 +258,7 @@
 
             @pl.when(active)
             def _():
+                to_mate(chip, s).wait_recv()
                 own[chip, s] = own[chip, s] + mate[chip, s]
 
                 @pl.when(jnp.where(side == 0, z > 0, z < chips - 1))
@@ -274,9 +277,9 @@
 
     lax.fori_loop(0, chips, chunk_step, 0)
     both_products(z)
-    to_mate(z).wait_recv()
 
     def last_step(s, carry):
+        to_mate(z, s).wait_recv()
         own[z, s] = own[z, s] + mate[z, s]
 
         @pl.when(z > 0)
@@ -350,8 +353,8 @@
     start_round(0)
     for node in range(per_col):
         low_ref[node] = tn(parent_ref[node], up_ref[node])
-    lax.fori_loop(per_col, combos, last_step, 0)
     for node in range(per_col):
+        last_step(per_col + node, 0)
         lower_term = jnp.zeros((width, width), jnp.float32)
         for place, span in spans():
             lower = own[z, per_col + node, :, span] - low_ref[node, :, span]
@@ -379,11 +382,10 @@
         ship((me_c + d) % n_col, me_c).wait_send()
         slot_copy((me_c + d) % n_col, me_c).wait_send()
     each_peer(lambda copy: copy.wait_send())
-    for chip in range(chips):
-        to_mate(chip).wait_send()
 
     def drain(i, carry):
         chip = i // combos
+        to_mate(chip, i % combos).wait_send()
 
         @pl.when(chip != z)
         def _():
@@ -509,8 +511,8 @@
             dma((n_row, n_col)),
             dma((n_row,)),
             dma((n_row,)),
-            dma((chips,)),
-            dma((chips,)),
+            dma((chips, combos)),
+            dma((chips, combos)),
             dma((chips, combos)),
             dma((chips + 1, combos)),
             dma((4, n_row)),
@@ -531,7 +533,7 @@
         out_shape=(wide, square, wide, square, square),
         in_specs=[pl.BlockSpec(memory_space=SMEM)] + [pl.BlockSpec(memory_space=VMEM)] * 6,
         out_specs=(pl.BlockSpec(memory_space=VMEM),) * 5,
-        compiler_params=pltpu.CompilerParams(vmem_limit_bytes=32 * 1024 * 1024),
+        compiler_params=pltpu.CompilerParams(vmem_limit_bytes=60 * 1024 * 1024),
         name="write_out",
     )(sorted_slots, upper_rows, lower_rows, totals, lower_parent, upper_dinv, lower_dinv)
 

time: 160 us -> 151 us (0.944)
  Pallas kernels: 154 us -> 148 us
  local copies, waits for them, and re-layouts: 3.68 us -> 0.6 us
    pallas_call x1, Pallas kernels: 151 us -> 145 us  [body(): pl.pallas_call(functools.partial(mega_kernel, per_col, n_row, n_col, len(...]
    unnamed x12 -> x2, local copies, waits for them, and re-layouts: 3.09 us -> 0.01 us
where the time goes in v4:
time: 151 us
  Pallas kernels  148 us (98%)
  other arithmetic  1.72 us (1%)
    pallas_call x1, Pallas kernels, body(): pl.pallas_call(functools.partial(mega_kernel, per_col, n_row, n_col, len(...  145 us
    pallas_call x1, Pallas kernels, body(): pl.pallas_call(functools.partial(write_kernel, row_blocks), out_shape=(wi...  3.46 us

profile of v4, /device:TPU:16, one launch (start us, length us, event | category | flops | bytes accessed | tf_op | source)
XLA Modules:
  0.0 151.3 jit_solution(10929729521535300631)
XLA Ops:
  0.6 0.9 select_reduce_fusion.2
  1.5 0.2 convert_reduce_fusion
  1.7 0.7 select_reduce_fusion
  2.4 0.0 copy-start
  2.4 0.6 pad.4.tile_ref
  3.0 144.8 %selected_inverse.1 = (f32[2,128,512]{2,1,0:T(8,128)}, f32[2,128,512]{2,1,0:T(8,128)}, f32[4,6,32,128]{3,2,1,0:T(8,128)}) custom-call(s32[2,16]{1,0:T(2,128)} %get-tuple-element.11.order_ref, s32[2]{0:T(128)} %up_len_ref.1, s32[2]{0:T(128)} %low_len_ref.1, s32[8,128]{1,0:T(8,128)} %pad.4.tile_ref, f32[2,4,128,128]{3,2,1,0:T(8,128)} %bitcast.2, ...), custom_call_target="tpu_custom_call" | custom-call | tf_op jit(solution)/shard_map/selected_inverse/pallas_call | solution.py:479
  147.8 0.0 copy-done
  147.8 3.5 %write_out.1 = (f32[2,128,1024]{2,1,0:T(8,128)}, f32[2,128,128]{2,1,0:T(8,128)}, f32[2,128,1024]{2,1,0:T(8,128)}, f32[2,128,128]{2,1,0:T(8,128)}, f32[2,128,128]{2,1,0:T(8,128)}) custom-call(s32[2,16]{1,0:T(2,128)} %copy-done, f32[2,128,512]{2,1,0:T(8,128)} %get-tuple-element.8.up_ref, f32[2,128,512]{2,1,0:T(8,128)} %get-tuple-element.9.low_ref, ...), custom_call_target="tpu_custom_call" | custom-call | tf_op jit(solution)/shard_map/write_out/pallas_call | solution.py:531
Async XLA Ops:
  2.4 145.4 %copy-start = (s32[2,16]{1,0:T(2,128)}, s32[2,16]{1,0:T(2,128)S(1)}, u32[]{:S(2)}) copy-start(s32[2,16]{1,0:T(2,128)S(1)} %get-tuple-element.12.slot_ref) | copy-start | bytes 388

commit v5 on v4

--- a/solution.py
+++ b/solution.py
@@ -294,8 +294,21 @@
 
         return carry
 
+    each_peer(lambda copy: copy.wait_send())
+    for d in range(1, n_col):
+        ship((me_c + d) % n_col, me_c).wait_send()
+        slot_copy((me_c + d) % n_col, me_c).wait_send()
+    for d in range(1, n_row):
+        local_copy((me_r + d) % n_row, me_r).wait_send()
+        for c in range(n_col):
+            pass_on(c, (me_r + d) % n_row, me_r).wait_send()
+    for chip in range(chips):
+        for s in range(combos):
+            to_mate(chip, s).wait_send()
+
     part_rows = width // n_row
-    rounds = ((0, 2 * per_col), (2 * per_col, per_col))
+    rounds = ((0, 2 * per_col),) + tuple((2 * per_col + node, 1) for node in range(per_col))
+    n_rounds = len(rounds)
 
     def full(combo, place):
         return jnp.concatenate([local[combo * parts + part, place] for part in range(parts)], axis=0)
@@ -317,8 +330,8 @@
 
     def spread_total(at, peer, source):
         part = pl.ds(*rounds[at])
-        return remote(totals.at[source, part], totals.at[source, part], t_send.at[2 + at, peer],
-                      t_recv.at[2 + at, source], {"row": peer})
+        return remote(totals.at[source, part], totals.at[source, part], t_send.at[n_rounds + at, peer],
+                      t_recv.at[n_rounds + at, source], {"row": peer})
 
     def start_round(at):
         for d in range(1, n_row):
@@ -362,30 +375,21 @@
             low_ref[node, :, span] = lower
             lower_term = lower_term + nt(full(per_col + node, place), lower)
         put(2, node, lower_term)
-    start_round(1)
-    sum_round(0)
-    sum_round(1)
-    for at in range(2):
+        start_round(1 + node)
+        sum_round(node)
+    sum_round(per_col)
+    for at in range(n_rounds):
         for d in range(1, n_row):
             spread_total(at, me_r, (me_r + d) % n_row).wait_recv()
     totals_ref[...] = totals[...]
 
     for d in range(1, n_row):
-        peer = (me_r + d) % n_row
-        local_copy(peer, me_r).wait_send()
-        for at in range(2):
-            scatter(at, peer, me_r).wait_send()
-            spread_total(at, peer, me_r).wait_send()
-        for c in range(n_col):
-            pass_on(c, peer, me_r).wait_send()
-    for d in range(1, n_col):
-        ship((me_c + d) % n_col, me_c).wait_send()
-        slot_copy((me_c + d) % n_col, me_c).wait_send()
-    each_peer(lambda copy: copy.wait_send())
+        for at in range(n_rounds):
+            scatter(at, (me_r + d) % n_row, me_r).wait_send()
+            spread_total(at, (me_r + d) % n_row, me_r).wait_send()
 
     def drain(i, carry):
         chip = i // combos
-        to_mate(chip, i % combos).wait_send()
 
         @pl.when(chip != z)
         def _():
@@ -515,8 +519,8 @@
             dma((chips, combos)),
             dma((chips, combos)),
             dma((chips + 1, combos)),
-            dma((4, n_row)),
-            dma((4, n_row)),
+            dma((2 * (1 + per_col), n_row)),
+            dma((2 * (1 + per_col), n_row)),
             dma((n_col,)),
             dma((n_col,)),
             dma(()),

time: 151 us -> 150 us (level)
  no operation moved by 1% of the time
where the time goes in v5:
time: 150 us
  Pallas kernels  147 us (98%)
  other arithmetic  1.72 us (1%)
    pallas_call x1, Pallas kernels, body(): pl.pallas_call(functools.partial(mega_kernel, per_col, n_row, n_col, len(...  143 us
    pallas_call x1, Pallas kernels, body(): pl.pallas_call(functools.partial(write_kernel, row_blocks), out_shape=(wi...  3.46 us

profile of v5, /device:TPU:16, one launch (start us, length us, event | category | flops | bytes accessed | tf_op | source)
XLA Modules:
  0.0 149.9 jit_solution(304686998627777088)
XLA Ops:
  0.6 0.9 select_reduce_fusion.2
  1.5 0.2 convert_reduce_fusion
  1.7 0.7 select_reduce_fusion
  2.4 0.0 copy-start
  2.4 0.6 pad.4.tile_ref
  3.0 143.5 %selected_inverse.1 = (f32[2,128,512]{2,1,0:T(8,128)}, f32[2,128,512]{2,1,0:T(8,128)}, f32[4,6,32,128]{3,2,1,0:T(8,128)}) custom-call(s32[2,16]{1,0:T(2,128)} %get-tuple-element.11.order_ref, s32[2]{0:T(128)} %up_len_ref.1, s32[2]{0:T(128)} %low_len_ref.1, s32[8,128]{1,0:T(8,128)} %pad.4.tile_ref, f32[2,4,128,128]{3,2,1,0:T(8,128)} %bitcast.2, ...), custom_call_target="tpu_custom_call" | custom-call | tf_op jit(solution)/shard_map/selected_inverse/pallas_call | solution.py:483
  146.4 0.0 copy-done
  146.4 3.5 %write_out.1 = (f32[2,128,1024]{2,1,0:T(8,128)}, f32[2,128,128]{2,1,0:T(8,128)}, f32[2,128,1024]{2,1,0:T(8,128)}, f32[2,128,128]{2,1,0:T(8,128)}, f32[2,128,128]{2,1,0:T(8,128)}) custom-call(s32[2,16]{1,0:T(2,128)} %copy-done, f32[2,128,512]{2,1,0:T(8,128)} %get-tuple-element.8.up_ref, f32[2,128,512]{2,1,0:T(8,128)} %get-tuple-element.9.low_ref, ...), custom_call_target="tpu_custom_call" | custom-call | tf_op jit(solution)/shard_map/write_out/pallas_call | solution.py:535
Async XLA Ops:
  2.4 144.1 %copy-start = (s32[2,16]{1,0:T(2,128)}, s32[2,16]{1,0:T(2,128)S(1)}, u32[]{:S(2)}) copy-start(s32[2,16]{1,0:T(2,128)S(1)} %get-tuple-element.12.slot_ref) | copy-start | bytes 388
